TPU v7x, 32 devices: a whole 2x2x4 slice. The times are simulated.
32 devices in a mesh: groups: 2 (over x), corpus: 8 (over z, y), replica: 2 (over core).
Axes of the slice: x: 2, y: 2, z: 4, core: 2. Of those that a mesh axis runs over, the one named last changes fastest.
Arguments:
- queries: bfloat16 [2048, 1024], P(('groups', 'corpus', 'replica')), parts along dimension 0, may hold values from -6 to 6
- codebook: bfloat16 [32, 1024], P('groups'), parts along dimension 0, may hold values from -0.1875 to 0.1875
- pq_codes: int32 [32768, 256], P(('groups', 'corpus')), parts along dimension 0, may hold values from 0 to 15
- full_rows: bfloat16 [32768, 1024], P(('groups', 'corpus')), parts along dimension 0, may hold values from -0.1875 to 0.1875
- probe_ids: int32 [16, 2, 8, 4], P('groups', 'replica', 'corpus'), parts along dimension 0, may hold values from 0 to 7, as said below
- probe_len: int32 [16, 2, 8], P('groups', 'replica', 'corpus'), parts along dimension 0, may hold values from 1 to 4, 16 in all within a row
- cand_shard: int32 [2048, 4, 4], P(('groups', 'corpus', 'replica')), parts along dimension 0, may hold values from 0 to 7, all different within a row; in each aligned block of 256 rows (0 to 255, 256 to 511, ..., all dimensions but the last counted through in order) at most 256 rows name the same one
- cand_row: int32 [2048, 4, 4], P(('groups', 'corpus', 'replica')), parts along dimension 0, may hold values from 0 to 2047
Outputs:
- approx_scores: bfloat16 [16, 2, 8, 4, 64, 256], P('groups', 'replica', 'corpus'), parts along dimension 0
- exact_scores: float32 [2048, 4, 4], P(('groups', 'corpus', 'replica')), parts along dimension 0
There are 2 independent parts, one for each index of `groups`. A program takes and returns all parts, laid end to end along the dimension named above; each array names one. Nothing has to cross between parts.
Inputs may be any that keep to these rules, and one draw needn't show every extreme that they name: `probe_ids`: each list names 4 different posting blocks of the shard. `cand_shard`: the 4 candidates of a group lie on different shards; among the candidates of one query block at most 256 lie on any one shard, and some shard holds exactly 256 of them.
All inputs are finite; a program needn't handle non-finite values. No bound on the sum of `probe_len` on one device may be relied on, other than what follows from the above.
Results may differ from a plain program's by a relative error of at most 0.001.
Values may be sent and summed in bfloat16 or wider, within the bound.
No kernel may reach another device: no remote copies, remote signals or barrier semaphores. Data moves between devices by JAX's collectives and lax.ppermute only.
A program may use at most 128 MiB of HBM per device.

v0:
```python
import jax
import jax.numpy as jnp
from jax import lax
from jax.sharding import PartitionSpec as P

B = 256


def decode_slab(pq_codes, codebook):
    code_count = pq_codes.shape[1]
    feature_count = codebook.shape[1]
    sub_width = feature_count // code_count
    owner = jnp.arange(feature_count, dtype=jnp.int32)[None, :] // sub_width
    expand = (owner == jnp.arange(code_count, dtype=jnp.int32)[:, None]).astype(jnp.bfloat16)
    widened = jnp.dot(pq_codes.astype(jnp.bfloat16), expand, preferred_element_type=jnp.float32)
    decoded = jnp.zeros(widened.shape, codebook.dtype)
    for centroid in range(codebook.shape[0]):
        decoded = jnp.where(widened == float(centroid), codebook[centroid][None, :], decoded)
    return decoded


def local(queries, codebook, pq_codes, full_rows, probe_ids, probe_len, cand_shard, cand_row):
    shards = lax.axis_size("corpus")
    query_rows, feature_count = queries.shape
    slab_rows = full_rows.shape[0]
    blocks_here = slab_rows // B
    probe_slots = probe_ids.shape[-1]
    decoded = decode_slab(pq_codes, codebook)
    decoded_blocks = decoded.reshape(blocks_here, B, feature_count)
    gathered = lax.all_gather(queries, "corpus", axis=0, tiled=True)
    group_size = 1
    while shards % (group_size * 2) == 0 and group_size * query_rows < 512:
        group_size = group_size * 2
    step_count = shards // group_size
    block_queries = gathered.reshape(step_count, group_size, query_rows, feature_count)
    block_probes = probe_ids.reshape(step_count, group_size, probe_slots)
    live_slots = jnp.arange(probe_slots, dtype=jnp.int32)[None, :] < probe_len.reshape(shards, 1)
    block_live = live_slots.reshape(step_count, group_size, probe_slots)

    def score_step(loop_state, inputs):
        step_queries, step_probes, step_live = inputs
        chosen = jnp.take(decoded_blocks, step_probes.reshape(group_size * probe_slots), axis=0)
        chosen = chosen.reshape(group_size, probe_slots, B, feature_count)
        picked = jnp.einsum(
            "gqd,gpbd->gpqb", step_queries, chosen, preferred_element_type=jnp.float32
        )
        masked = jnp.where(step_live[:, :, None, None], picked, 0.0).astype(jnp.bfloat16)
        return (loop_state, masked)

    unused, approx_blocks = lax.scan(
        score_step, jnp.int32(0), (block_queries, block_probes, block_live)
    )
    approx_scores = approx_blocks.reshape(shards, 1, 1, probe_slots, query_rows, B)
    per_query = cand_shard.shape[1] * cand_shard.shape[2]
    cand_total = query_rows * per_query
    capacity = 2 * cand_total // shards
    target = cand_shard.reshape(cand_total)
    local_row = cand_row.reshape(cand_total)
    owner_query = jnp.arange(cand_total, dtype=jnp.int32) // per_query
    matches = (target[:, None] == jnp.arange(shards, dtype=jnp.int32)[None, :]).astype(jnp.bfloat16)
    order_index = jnp.arange(cand_total, dtype=jnp.int32)
    lower = (order_index[None, :] < order_index[:, None]).astype(jnp.bfloat16)
    earlier = jnp.dot(lower, matches, preferred_element_type=jnp.float32)
    send_slot = jnp.sum(earlier * matches.astype(jnp.float32), axis=1).astype(jnp.int32)
    position = target * capacity + send_slot
    placement_table = (
        position[:, None] == jnp.arange(shards * capacity, dtype=jnp.int32)[None, :]
    ).astype(jnp.float32)
    request_pair = jnp.stack(
        [local_row.astype(jnp.float32), owner_query.astype(jnp.float32)], axis=0
    )
    placed = jnp.dot(request_pair, placement_table, precision=lax.Precision.HIGHEST).astype(
        jnp.int32
    )
    request_rows = placed[0].reshape(shards, capacity)
    request_query = placed[1].reshape(shards, capacity)
    wanted_rows, wanted_query = (
        lax.all_to_all(request_rows, "corpus", split_axis=0, concat_axis=0, tiled=True),
        lax.all_to_all(request_query, "corpus", split_axis=0, concat_axis=0, tiled=True),
    )
    outgoing = jnp.take(full_rows, wanted_rows.reshape(shards * capacity), axis=0).reshape(
        shards, capacity, feature_count
    )
    arrived = lax.all_to_all(outgoing, "corpus", split_axis=0, concat_axis=0, tiled=True)
    fetched = jnp.take(arrived.reshape(shards * capacity, feature_count), position, axis=0)
    fetched = fetched.reshape(query_rows, per_query, feature_count)
    exact_values = jnp.einsum("qcd,qd->qc", fetched, queries, preferred_element_type=jnp.float32)
    exact_scores = exact_values.reshape(cand_shard.shape)
    return (approx_scores, exact_scores)


def solution(mesh):
    return jax.shard_map(
        local,
        mesh=mesh,
        in_specs=(
            P(("groups", "corpus", "replica"), None),
            P("groups", None),
            P(("groups", "corpus"), None),
            P(("groups", "corpus"), None),
            P("groups", "replica", "corpus", None),
            P("groups", "replica", "corpus"),
            P(("groups", "corpus", "replica"), None, None),
            P(("groups", "corpus", "replica"), None, None),
        ),
        out_specs=(
            P("groups", "replica", "corpus", None, None, None),
            P(("groups", "corpus", "replica"), None, None),
        ),
        check_vma=False,
    )
```

profile of v0, /device:TPU:0, one launch (start us, length us, event | category | flops | bytes accessed | tf_op | source)
XLA Modules:
  0.0 179.7 jit_solution(1233768666947834191)
XLA Ops:
  7.2 0.8 copy.35
  8.0 0.2 reshape.271
  8.2 0.5 fusion.17
  8.7 0.7 convert_element_type.74
  9.4 0.1 copy.38
  9.5 0.2 convert_element_type.75
  9.7 2.8 %fusion.4 = f32[2,2048]{1,0:T(2,128)S(1)} fusion(s32[1024]{0:T(1024)S(1)} %multiply_add_fusion, f32[1,1024]{1,0:T(1,128)S(1)} %fusion.34, f32[1,1024]{1,0:T(1,128)S(1)} %convert_element_type.75), kind=kOutput, calls=%fused_computation.24 | convolution fusion | flops 52430848 | bytes 28672 | tf_op jit(solution)/shard_map/dot_general | solution.py:72
  12.5 13.6 %all_to_all.14 = s32[8,1,256]{2,1,0:T(1,128)S(1)} all-to-all(s32[8,1,256]{2,1,0:T(1,128)S(1)} %bitcast.56), channel_id=1, replica_groups=mesh['groups'=2,'corpus'=8,'replica'=2] {'corpus'}, dimensions={0} | all-to-all | bytes 16384 | tf_op jit(solution)/shard_map/all_to_all | solution.py:78
  26.1 13.7 %gather_fusion.1 = bf16[2048,1024]{1,0:T(8,128)(2,1)} fusion(bf16[2048,1024]{1,0:T(8,128)(2,1)} %param.11, s32[2048]{0:T(1024)S(1)} %broadcast_clamp_fusion), kind=kCustom, calls=%fused_computation.1 | custom fusion | bytes 8396800 | tf_op jit(solution)/shard_map/jit(_take)/gather | solution.py:81
  39.8 3.8 %broadcast_select_fusion = bf16[8,256,1024]{2,1,0:T(8,128)(2,1)} fusion(bf16[8,256,1024]{2,1,0:T(8,128)(2,1)} %bitcast.49, pred[8,256]{1,0:T(8,128)(4,1)S(1)} %compare_and_fusion), kind=kLoop, calls=%fused_computation.28 | loop fusion | flops 2097152 | bytes 8390656 | tf_op jit(solution)/shard_map/jit(_take)/select_n | solution.py:81
  43.7 0.0 copy-start
  43.7 0.0 copy-start.4
  43.7 4.7 %all-to-all-start.1 = ((bf16[8,256,1024]{2,1,0:T(8,128)(2,1)}), bf16[8,256,1024]{2,1,0:T(8,128)(2,1)}, u32[]{:S(2)}, u32[]{:S(2)}) async-start(bf16[8,256,1024]{2,1,0:T(8,128)(2,1)} %broadcast_select_fusion), calls=%async_computation.1 | async-start | bytes 8388608 | tf_op jit(solution)/shard_map/all_to_all | solution.py:84
  48.4 0.2 all-gather.2.cloned.1.call-start
  48.6 0.5 all-gather.2.cloned.1.call-update
  49.1 0.0 copy-done
  49.1 0.2 slice_reduce_fusion.15
  49.3 0.0 copy-done.4
  49.3 19.4 %bitcast_select_fusion = bf16[2048,1024]{0,1:T(8,128)(2,1)} fusion(bf16[1024]{0:T(1024)(128)(2,1)S(1)} %get-tuple-element.41, bf16[1024]{0:T(1024)(128)(2,1)S(1)} %get-tuple-element.40, bf16[1024]{0:T(1024)(128)(2,1)S(1)} %get-tuple-element.39, bf16[1024]{0:T(1024)(128)(2,1)S(1)} %get-tuple-element.38, bf16[1024]{0:T(1024)(128)(2,1)S(1)} %get-tuple-element.37, ...), kind=kOutput, calls=%fused_computation.8 | convolution fusion | flops 1141899264 | bytes 6328320 | tf_op jit(solution)/shard_map/dot_general | solution.py:15
  68.7 0.0 copy-start.3
  68.7 0.0 copy-start.2
  68.7 6.5 %copy.45 = bf16[2048,1024]{1,0:T(8,128)(2,1)} copy(bf16[2048,1024]{0,1:T(8,128)(2,1)} %bitcast_select_fusion) | data formatting | bytes 8388608 | tf_op jit(solution)/shard_map/reshape | solution.py:29
  75.2 0.0 copy-done.3
  75.2 0.1 copy.33
  75.3 0.1 reshape.269
  75.4 0.1 copy.32
  75.5 0.0 copy-done.2
  75.5 0.1 copy.40
  75.6 0.2 mul.38
  75.8 0.1 convert_element_type.73
  75.9 0.1 copy.36
  76.0 0.1 copy.37
  76.1 0.0 copy-start.5
  76.1 9.3 %gather_fusion = bf16[32,256,1024]{2,1,0:T(8,128)(2,1)} fusion(bf16[8,256,1024]{2,1,0:T(8,128)(2,1)} %bitcast.48, s32[1024]{0:T(1024)S(1)} %pad_clamp_fusion), kind=kCustom, calls=%fused_computation | custom fusion | bytes 33554560 | tf_op jit(solution)/shard_map/while/body/eval_jaxpr/jit(_take)/gather | solution.py:42
  85.4 0.0 copy-done.5
  85.4 0.1 iota_compare_fusion.11
  85.5 68.1 %all-gather.2.cloned.1.call-done = bf16[512,1024]{1,0:T(8,128)(2,1)} async-done(((bf16[64,1024]{1,0:T(8,128)(2,1)}), bf16[512,1024]{1,0:T(8,128)(2,1)}) %all-gather.2.cloned.1.call-update) | async-done | bytes 1048592 | tf_op jit(solution)/shard_map/all_gather | solution.py:30
  153.6 9.9 %fusion.13 = bf16[8,1,1,4,64,256]{5,4,3,2,1,0:T(8,128)(2,1)} fusion(bf16[8,64,1024,1]{2,1,3,0:T(8,128)(2,1)} %bitcast.60, bf16[8,4,256,1024]{3,2,1,0:T(8,128)(2,1)} %bitcast.50, pred[8,4]{1,0:T(8,128)(4,1)S(1)} %copy.32, pred[8,4]{1,0:T(8,128)(4,1)S(1)} %iota_compare_fusion.11), kind=kOutput, calls=%fused_computation.34 | convolution fusion | flops 1083179008 | bytes 18874432 | tf_op jit(solution)/shard_map/while/body/eval_jaxpr/gqd,gpbd->gpqb/dot_general | solution.py:44
  163.5 0.0 all-to-all-done.1
  163.5 0.0 copy-start.1
  163.5 7.7 %gather_fusion.2 = bf16[1024,1024]{1,0:T(8,128)(2,1)S(1)} fusion(bf16[2048,1024]{1,0:T(8,128)(2,1)} %bitcast.18, s32[1024]{0:T(1024)S(1)} %broadcast_clamp_fusion.1), kind=kCustom, calls=%fused_computation.2 | custom fusion | bytes 4198400 | tf_op jit(solution)/shard_map/jit(_take)/gather | solution.py:85
  171.3 0.0 copy-done.1
  171.3 0.9 fusion.8
  172.2 0.7 copy.44
  (15 shorter events, 0.1 us)
Async XLA Ops:
  43.7 5.4 %copy-start = (bf16[16,1024]{1,0:T(8,128)(2,1)S(1)}, bf16[16,1024]{1,0:T(8,128)(2,1)}, u32[]{:S(2)}) copy-start(bf16[16,1024]{1,0:T(8,128)(2,1)} %param.9) | copy-start | bytes 98308
  43.7 5.6 %copy-start.4 = (s32[2048,256]{1,0:T(8,128)S(1)}, s32[2048,256]{1,0:T(8,128)}, u32[]{:S(2)}) copy-start(s32[2048,256]{1,0:T(8,128)} %param.10) | copy-start | bytes 6291460
  43.7 119.8 %all-to-all-start.1 = ((bf16[8,256,1024]{2,1,0:T(8,128)(2,1)}), bf16[8,256,1024]{2,1,0:T(8,128)(2,1)}, u32[]{:S(2)}, u32[]{:S(2)}) async-start(bf16[8,256,1024]{2,1,0:T(8,128)(2,1)} %broadcast_select_fusion), calls=%async_computation.1 | async-start | bytes 8388608 | tf_op jit(solution)/shard_map/all_to_all | solution.py:84
  48.4 105.3 %all-gather.2.cloned.1.call-start = ((), (), s32[]{:S(2)}) async-start(), calls=%async_computation.2 | async-start | bytes 1179648 | tf_op jit(solution)/shard_map/all_gather | solution.py:30
  68.7 6.5 %copy-start.3 = (s32[8,1,1,4]{0,3,2,1:T(4,128)S(1)}, s32[8,1,1,4]{0,3,2,1:T(4,128)}, u32[]{:S(2)}) copy-start(s32[8,1,1,4]{0,3,2,1:T(4,128)} %param.12) | copy-start | bytes 388
  68.7 6.7 %copy-start.2 = (s32[64,4,4]{0,2,1:T(4,128)S(1)}, s32[64,4,4]{0,2,1:T(4,128)}, u32[]{:S(2)}) copy-start(s32[64,4,4]{0,2,1:T(4,128)} %param.14) | copy-start | bytes 12292
  76.1 9.4 %copy-start.5 = (s32[8,1,1]{0,2,1:T(1,128)S(1)}, s32[8,1,1]{0,2,1:T(1,128)}, u32[]{:S(2)}) copy-start(s32[8,1,1]{0,2,1:T(1,128)} %param.13) | copy-start | bytes 100
  163.5 7.8 %copy-start.1 = (bf16[64,1024]{1,0:T(8,128)(2,1)S(1)}, bf16[64,1024]{1,0:T(8,128)(2,1)}, u32[]{:S(2)}) copy-start(bf16[64,1024]{1,0:T(8,128)(2,1)} %param.8) | copy-start | bytes 393220
Sparse Core Ops, SparseCore 0:
  51.3 102.2 all-gather.1
where the time goes:
time: 180 us
  waiting for transfers between devices  68.6 us (38%)
  local copies, waits for them, and re-layouts  40.2 us (22%)
  matrix products  33.5 us (19%)
  between operations  14.2 us (8%)
  blocking collectives  13.6 us (8%)
  starting transfers between devices  4.9 us (3%)
  other arithmetic  4.72 us (3%)
    all_gather x1, waiting for transfers between devices, local(): gathered = lax.all_gather(queries, 'corpus', axis=0, tiled=True)  68.1 us
    dot_general x1, matrix products, decode_slab(): jnp.dot(pq_codes.astype(jnp.bfloat16), expand, preferred_element_type=jnp...  19.4 us
    gather x1, local copies, waits for them, and re-layouts, local(): jnp.take(full_rows, wanted_rows.reshape(shards * capacity), axis=0)  13.7 us
    all_to_all x1, blocking collectives, local(): lax.all_to_all(request_rows, 'corpus', split_axis=0, concat_axis=0, tiled...  13.6 us
    dot_general x1, matrix products, score_step(): jnp.einsum('gqd,gpbd->gpqb', step_queries, chosen, preferred_element_type...  9.88 us
    gather x1, local copies, waits for them, and re-layouts, score_step(): jnp.take(decoded_blocks, step_probes.reshape(group_size * probe_slots), a...  9.34 us
    gather x1, local copies, waits for them, and re-layouts, local(): jnp.take(arrived.reshape(shards * capacity, feature_count), position, axi...  7.74 us
    reshape x1, local copies, waits for them, and re-layouts, local(): decoded_blocks = decoded.reshape(blocks_here, B, feature_count)  6.45 us
  transfers between devices with their start and end apart: 2, of which 1 were waited for; matrix products, arithmetic and copies ran while one was open for 26% of the time, Pallas kernels for 0%

commit v1 on v0

v1 whole, which is shorter than its diff:
```python
import functools

import jax
import jax.numpy as jnp
from jax import lax
from jax.experimental import pallas as pl
from jax.experimental.pallas import tpu as pltpu
from jax.sharding import PartitionSpec as P

B = 256
NT = (((1,), (1,)), ((), ()))
IN_VMEM = pl.BlockSpec(memory_space=pltpu.VMEM)
IN_SMEM = pl.BlockSpec(memory_space=pltpu.SMEM)
LIMIT = 24 * 2**20


def params():
    return pltpu.CompilerParams(vmem_limit_bytes=LIMIT)


def pick(table, index):
    return jnp.take_along_axis(table, index, axis=0, mode="promise_in_bounds")


def decode_kernel(codes_ref, book_ref, out_ref, expand_ref, *, sub_width, step):
    rows, code_count = codes_ref.shape
    features = book_ref.shape[1]
    owner = lax.broadcasted_iota(jnp.int32, (code_count, features), 1) // sub_width
    place = lax.broadcasted_iota(jnp.int32, (code_count, features), 0)
    expand_ref[...] = (owner == place).astype(jnp.bfloat16)

    @pl.loop(0, rows // step)
    def _(at):
        here = pl.ds(pl.multiple_of(at * step, step), step)
        codes = codes_ref[here, :].astype(jnp.bfloat16)
        for left in range(0, features, 128):
            lanes = slice(left, left + 128)
            if left % 256 == 0:
                wide = jnp.dot(
                    codes, expand_ref[:, left : left + 256], preferred_element_type=jnp.float32
                ).astype(jnp.int32)
            centroids = book_ref[:, lanes].astype(jnp.float32)
            low, high = centroids[:8], centroids[8:]
            pieces = []
            for top in range(0, step, 8):
                index = wide[top : top + 8, left % 256 : left % 256 + 128]
                inner = index & 7
                pieces.append(jnp.where(index >= 8, pick(high, inner), pick(low, inner)))
            out_ref[here, lanes] = jnp.concatenate(pieces, axis=0).astype(jnp.bfloat16)


def decode(pq_codes, codebook):
    rows, code_count = pq_codes.shape
    features = codebook.shape[1]
    return pl.pallas_call(
        functools.partial(decode_kernel, sub_width=features // code_count, step=256),
        out_shape=jax.ShapeDtypeStruct((rows, features), jnp.bfloat16),
        in_specs=[IN_VMEM, IN_VMEM],
        out_specs=IN_VMEM,
        scratch_shapes=[pltpu.VMEM((code_count, features), jnp.bfloat16)],
        compiler_params=params(),
        cost_estimate=pl.CostEstimate(
            flops=2 * rows * code_count * features, bytes_accessed=8 * 2**20, transcendentals=0
        ),
        name="decode",
    )(pq_codes, codebook)


def exact_kernel(base_ref, cand_ref, rows_ref, *refs, places, groups):
    blocks, outs, stack = refs[: len(places)], refs[len(places) : -1], refs[-1]
    query_rows = blocks[0].shape[0]
    row_count = rows_ref.shape[0]
    per_query = cand_ref.shape[0]
    tops = per_query // groups
    for at, block in enumerate(blocks):
        stack[at * query_rows : (at + 1) * query_rows, :] = block[...]
    width = len(blocks) * query_rows
    scores = lax.dot_general(
        rows_ref[...], stack[...], NT, preferred_element_type=jnp.float32
    )
    wanted = (
        jnp.concatenate(
            [cand_ref[:, p * query_rows : (p + 1) * query_rows] for p in places], axis=1
        )
        - base_ref[0]
    )
    mine = (wanted >= 0) & (wanted < row_count)
    kept = jnp.where(mine, wanted, -1)
    down = lax.broadcasted_iota(jnp.int32, (8, width), 0)
    found = []
    for group in range(groups):
        row = jnp.max(kept[group * tops : (group + 1) * tops], axis=0, keepdims=True)
        row = jnp.broadcast_to(row, (8, width)) - down
        total = jnp.zeros((8, width), jnp.float32)
        for top in range(0, row_count, 8):
            total = jnp.where(row == top, scores[top : top + 8], total)
        total = jnp.sum(total, axis=0, keepdims=True)
        found.append(jnp.broadcast_to(total, (tops, width)))
    answer = jnp.where(mine, jnp.concatenate(found, axis=0), 0.0)
    for at, out in enumerate(outs):
        out[...] = answer[:, at * query_rows : (at + 1) * query_rows]


def exact(base, cands, full_rows, blocks, places, groups):
    query_rows, features = blocks[0].shape
    per_query = cands.shape[0]
    count = len(blocks)
    return pl.pallas_call(
        functools.partial(exact_kernel, places=places, groups=groups),
        out_shape=[jax.ShapeDtypeStruct((per_query, query_rows), jnp.float32)] * count,
        in_specs=[IN_SMEM] + [IN_VMEM] * (2 + count),
        out_specs=[IN_VMEM] * count,
        scratch_shapes=[pltpu.VMEM((count * query_rows, features), jnp.bfloat16)],
        compiler_params=params(),
        cost_estimate=pl.CostEstimate(
            flops=2 * count * query_rows * features * full_rows.shape[0],
            bytes_accessed=4 * 2**20,
            transcendentals=0,
        ),
        name="exact",
    )(base, cands, full_rows, *blocks)


def approx_kernel(where_ref, ids_ref, len_ref, rows_ref, *refs):
    blocks, out_ref, stack, scores = refs[:-3], refs[-3], refs[-2], refs[-1]
    query_rows = blocks[0].shape[0]
    slots = out_ref.shape[1]
    for at, block in enumerate(blocks):
        stack[at * query_rows : (at + 1) * query_rows, :] = block[...]
    for block in range(scores.shape[0]):
        scores[block] = lax.dot_general(
            stack[...],
            rows_ref[block * B : (block + 1) * B, :],
            NT,
            preferred_element_type=jnp.float32,
        ).astype(jnp.bfloat16)

    for at in range(len(blocks)):
        owner = where_ref[at]
        here = slice(at * query_rows, (at + 1) * query_rows)
        for slot in range(slots):
            picked = scores[ids_ref[owner, slot], here, :]
            out_ref[owner, slot] = jnp.where(slot < len_ref[owner], picked, jnp.zeros_like(picked))


def approx(where, probe_ids, probe_len, decoded, blocks):
    query_rows, features = blocks[0].shape
    count = len(blocks)
    slots = probe_ids.shape[1]
    block_count = decoded.shape[0] // B
    width = count * query_rows
    return pl.pallas_call(
        approx_kernel,
        out_shape=jax.ShapeDtypeStruct((count, slots, query_rows, B), jnp.bfloat16),
        in_specs=[IN_SMEM] * 3 + [IN_VMEM] * (1 + count),
        out_specs=IN_VMEM,
        scratch_shapes=[
            pltpu.VMEM((width, features), jnp.bfloat16),
            pltpu.VMEM((block_count, width, B), jnp.bfloat16),
        ],
        compiler_params=params(),
        cost_estimate=pl.CostEstimate(
            flops=2 * width * features * decoded.shape[0],
            bytes_accessed=4 * 2**20,
            transcendentals=0,
        ),
        name="approx",
    )(where, probe_ids, probe_len, decoded, *blocks)


def swap(x, distance, shards):
    return lax.ppermute(x, "corpus", [(i, i ^ distance) for i in range(shards)])


def local(queries, codebook, pq_codes, full_rows, probe_ids, probe_len, cand_shard, cand_row):
    shards = lax.axis_size("corpus")
    me = lax.axis_index("corpus")
    query_rows, features = queries.shape
    slab_rows = full_rows.shape[0]
    groups, tops = cand_shard.shape[1:]
    per_query = groups * tops
    slots = probe_ids.shape[-1]
    base = (me * slab_rows).astype(jnp.int32).reshape(1)
    ids = probe_ids.reshape(shards, slots)
    lens = probe_len.reshape(shards)
    wanted = (cand_shard * slab_rows + cand_row).reshape(query_rows, per_query).T

    if shards == 8:
        far = swap(queries, 4, shards)
        near = swap(queries, 2, shards)
        side = swap(queries, 1, shards)
        cross = swap(queries, 7, shards)
        near_side = swap(near, 1, shards)
        far_near = swap(far, 2, shards)
        far_side = swap(far, 1, shards)
        blocks = [queries, side, near, near_side, far, far_side, far_near, cross]
        for distance in (1, 2, 4):
            wanted = jnp.concatenate([wanted, swap(wanted, distance, shards)], axis=1)
        decoded = decode(pq_codes, codebook)
        places = list(range(8))
        answers = exact(base, wanted, full_rows, blocks, places, groups)
        back = [answers[0]] + [swap(answers[p], p, shards) for p in places[1:]]
        where = me ^ jnp.arange(8, dtype=jnp.int32)
        approx_scores = approx(where, ids, lens, decoded, blocks)
        total = functools.reduce(jnp.add, back)
    else:
        gathered = lax.all_gather(queries, "corpus", axis=0)
        asked = lax.all_gather(wanted, "corpus", axis=0)
        decoded = decode(pq_codes, codebook)
        answers, pieces = [], []
        step = 4
        for first in range(0, shards, step):
            picked = list(range(first, first + step))
            cands = jnp.concatenate([asked[p] for p in picked], axis=1)
            answers += exact(
                base, cands, full_rows, [gathered[p] for p in picked], list(range(step)), groups
            )
            pieces.append(
                approx(
                    jnp.arange(step, dtype=jnp.int32),
                    ids[first : first + step],
                    lens[first : first + step],
                    decoded,
                    [gathered[p] for p in picked],
                )
            )
        approx_scores = jnp.concatenate(pieces, axis=0)
        back = lax.all_to_all(jnp.stack(answers), "corpus", 0, 0, tiled=True)
        total = jnp.sum(back, axis=0)

    approx_scores = approx_scores.reshape(shards, 1, 1, slots, query_rows, B)
    return approx_scores, total.T.reshape(query_rows, groups, tops)


def solution(mesh):
    return jax.shard_map(
        local,
        mesh=mesh,
        in_specs=(
            P(("groups", "corpus", "replica"), None),
            P("groups", None),
            P(("groups", "corpus"), None),
            P(("groups", "corpus"), None),
            P("groups", "replica", "corpus", None),
            P("groups", "replica", "corpus"),
            P(("groups", "corpus", "replica"), None, None),
            P(("groups", "corpus", "replica"), None, None),
        ),
        out_specs=(
            P("groups", "replica", "corpus", None, None, None),
            P(("groups", "corpus", "replica"), None, None),
        ),
        check_vma=False,
    )
```

time: 180 us -> 58.2 us (0.32)
  waiting for transfers between devices: 68.6 us -> 9.14 us
  matrix products: 33.5 us -> 0 us
  local copies, waits for them, and re-layouts: 40.2 us -> 7.31 us
  starting transfers between devices: 4.9 us -> 27.1 us
  blocking collectives: 13.6 us -> 0 us
  between operations: 14.2 us -> 0.73 us
  Pallas kernels: 0 us -> 12 us
  other arithmetic: 4.72 us -> 1.7 us
    all_gather x1 -> x0, waiting for transfers between devices: 68.1 us -> none  [local(): gathered = lax.all_gather(queries, 'corpus', axis=0, tiled=True)]
    dot_general x5 -> x0, matrix products: 33.5 us -> none  [the longest x1 19.4 us: decode_slab(): jnp.dot(pq_codes.astype(jnp.bfloat16), expand, preferred_element_type=jnp...]
    gather x3 -> x0, local copies, waits for them, and re-layouts: 30.8 us -> none  [the longest x1 13.7 us: local(): jnp.take(full_rows, wanted_rows.reshape(shards * capacity), axis=0)]
    ppermute x0 -> x17, starting transfers between devices: none -> 27.1 us  [swap(): return lax.ppermute(x, 'corpus', [(i, i ^ distance) for i in range(shards)])]
    all_to_all x1 -> x0, blocking collectives: 13.6 us -> none  [local(): lax.all_to_all(request_rows, 'corpus', split_axis=0, concat_axis=0, tiled...]
    pallas_call x0 -> x3, Pallas kernels: none -> 12 us  [the longest x1 4.68 us: decode(): pl.pallas_call(functools.partial(decode_kernel, sub_width=features // cod...]
    ppermute x0 -> x17, waiting for transfers between devices: none -> 9.14 us  [swap(): return lax.ppermute(x, 'corpus', [(i, i ^ distance) for i in range(shards)])]
    reshape x3 -> x1, local copies, waits for them, and re-layouts: 6.69 us -> 0.08 us  [local(): ids = probe_ids.reshape(shards, slots)]
  transfers between devices with their start and end apart: 2 -> 17, of which waited for: 1 -> 4; matrix products, arithmetic and copies ran while one was open for 26% -> 0% of each run, Pallas kernels for 0% -> 15%
where the time goes in v1:
time: 58.2 us; the launch traced here: 58 us
  starting transfers between devices  27.1 us (47%)
  Pallas kernels  12 us (21%)
  waiting for transfers between devices  9.14 us (16%)
  local copies, waits for them, and re-layouts  7.31 us (13%)
  other arithmetic  1.7 us (3%)
  between operations  0.73 us (1%)
    ppermute x17, starting transfers between devices, swap(): return lax.ppermute(x, 'corpus', [(i, i ^ distance) for i in range(shards)])  27.1 us
    ppermute x17, waiting for transfers between devices, swap(): return lax.ppermute(x, 'corpus', [(i, i ^ distance) for i in range(shards)])  9.14 us
    unnamed x18, local copies, waits for them, and re-layouts  7.23 us
    pallas_call x1, Pallas kernels, decode(): pl.pallas_call(functools.partial(decode_kernel, sub_width=features // cod...  4.68 us
    pallas_call x1, Pallas kernels, approx(): pl.pallas_call(approx_kernel, out_shape=jax.ShapeDtypeStruct((count, slot...  4.07 us
    pallas_call x1, Pallas kernels, exact(): pl.pallas_call(functools.partial(exact_kernel, places=places, groups=grou...  3.23 us
  transfers between devices with their start and end apart: 17, of which 4 were waited for; matrix products, arithmetic and copies ran while one was open for 0% of the time, Pallas kernels for 15%

profile of v1, /device:TPU:0, one launch (start us, length us, event | category | flops | bytes accessed | tf_op | source)
XLA Modules:
  0.0 58.0 jit_solution(13958854767356699990)
XLA Ops:
  0.6 0.0 copy-start.2
  0.6 0.0 copy-start.3
  0.7 0.9 %multiply_add_fusion = s32[64,4,4]{0,2,1:T(4,128)S(1)} fusion(s32[64,4,4]{0,2,1:T(4,128)} %param.15, s32[64,4,4]{0,2,1:T(4,128)} %param.14), kind=kLoop, calls=%fused_computation.4 | loop fusion | flops 2048 | bytes 12288 | tf_op jit(solution)/shard_map/add | solution.py:186
  1.5 3.0 %collective-permute-start.7 = (s32[16,64]{1,0:T(8,128)S(1)}, s32[16,64]{1,0:T(8,128)S(1)}, u32[]{:S(2)}, u32[]{:S(2)}) collective-permute-start(s32[16,64]{1,0:T(8,128)S(1)} %bitcast.13), channel_id=1, source_target_pairs={{0,2},{2,0},{4,6},{6,4},{8,10},{10,8},{12,14},{14,12},{1,3},{3,1},... | collective-permute-start | bytes 12296 | tf_op jit(solution)/shard_map/ppermute | solution.py:172
  4.5 1.6 %collective-permute-done.7 = s32[16,64]{1,0:T(8,128)S(1)} collective-permute-done((s32[16,64]{1,0:T(8,128)S(1)}, s32[16,64]{1,0:T(8,128)S(1)}, u32[]{:S(2)}, u32[]{:S(2)}) %collective-permute-start.7) | collective-permute-done | bytes 4128 | tf_op jit(solution)/shard_map/ppermute | solution.py:172
  6.1 0.1 pad_add_fusion.2
  6.2 2.1 %collective-permute-start.8 = (s32[16,128]{1,0:T(8,128)S(1)}, s32[16,128]{1,0:T(8,128)S(1)}, u32[]{:S(2)}, u32[]{:S(2)}) collective-permute-start(s32[16,128]{1,0:T(8,128)S(1)} %pad_add_fusion.2), channel_id=1, source_target_pairs={{0,4},{2,6},{4,0},{6,2},{8,12},{10,14},{12,8},{14,10},{1,5},{3,7},... | collective-permute-start | bytes 24584 | tf_op jit(solution)/shard_map/ppermute | solution.py:172
  8.3 2.6 %collective-permute-start.3 = (bf16[64,1024]{1,0:T(8,128)(2,1)}, bf16[64,1024]{1,0:T(8,128)(2,1)S(1)}, u32[]{:S(2)}, u32[]{:S(2)}) collective-permute-start(bf16[64,1024]{1,0:T(8,128)(2,1)} %refs_0_.3), channel_id=1, source_target_pairs={{0,8},{2,10},{4,12},{6,14},{8,0},{10,2},{12,4},{14,6},{1,9},{3,11}... | collective-permute-start | bytes 393224 | tf_op jit(solution)/shard_map/ppermute | solution.py:172
  10.9 0.4 collective-permute-start.1
  11.3 0.0 collective-permute-done.8
  11.3 0.1 pad_add_fusion.1
  11.4 1.8 %collective-permute-start.9 = (s32[16,256]{1,0:T(8,128)S(1)}, s32[16,256]{1,0:T(8,128)S(1)}, u32[]{:S(2)}, u32[]{:S(2)}) collective-permute-start(s32[16,256]{1,0:T(8,128)S(1)} %pad_add_fusion.1), channel_id=1, source_target_pairs={{0,8},{2,10},{4,12},{6,14},{8,0},{10,2},{12,4},{14,6},{1,9},{3,11}... | collective-permute-start | bytes 49160 | tf_op jit(solution)/shard_map/ppermute | solution.py:172
  13.2 1.5 %collective-permute-start = (bf16[64,1024]{1,0:T(8,128)(2,1)}, bf16[64,1024]{1,0:T(8,128)(2,1)S(1)}, u32[]{:S(2)}, u32[]{:S(2)}) collective-permute-start(bf16[64,1024]{1,0:T(8,128)(2,1)} %refs_0_.3), channel_id=1, source_target_pairs={{0,2},{2,0},{4,6},{6,4},{8,10},{10,8},{12,14},{14,12},{1,3},{3,1},... | collective-permute-start | bytes 393224 | tf_op jit(solution)/shard_map/ppermute | solution.py:172
  14.7 2.1 %collective-permute-start.6 = (bf16[64,1024]{1,0:T(8,128)(2,1)}, bf16[64,1024]{1,0:T(8,128)(2,1)S(1)}, u32[]{:S(2)}, u32[]{:S(2)}) collective-permute-start(bf16[64,1024]{1,0:T(8,128)(2,1)} %refs_0_.3), channel_id=1, source_target_pairs={{0,14},{2,12},{4,10},{6,8},{8,6},{10,4},{12,2},{14,0},{1,15},{3,13... | collective-permute-start | bytes 393224 | tf_op jit(solution)/shard_map/ppermute | solution.py:172
  16.8 1.8 %collective-permute-done.3.refs_4_ = bf16[64,1024]{1,0:T(8,128)(2,1)S(1)} collective-permute-done((bf16[64,1024]{1,0:T(8,128)(2,1)}, bf16[64,1024]{1,0:T(8,128)(2,1)S(1)}, u32[]{:S(2)}, u32[]{:S(2)}) %collective-permute-start.3) | collective-permute-done | bytes 131104 | tf_op jit(solution)/shard_map/ppermute | solution.py:172
  18.6 1.6 %collective-permute-start.4 = (bf16[64,1024]{1,0:T(8,128)(2,1)S(1)}, bf16[64,1024]{1,0:T(8,128)(2,1)S(1)}, u32[]{:S(2)}, u32[]{:S(2)}) collective-permute-start(bf16[64,1024]{1,0:T(8,128)(2,1)S(1)} %collective-permute-done.3.refs_4_), channel_id=1, source_target_pairs={{0,2},{2,0},{4,6},{6,4},{8,10},{10,8},{12,14},{14,12},{1,3},{3,1},... | collective-permute-start | bytes 393224 | tf_op jit(solution)/shard_map/ppermute | solution.py:172
  20.2 0.0 collective-permute-done.9
  20.2 0.0 collective-permute-start.5
  20.2 0.0 collective-permute-done.1.refs_2_
  20.2 0.8 %collective-permute-start.2 = (bf16[64,1024]{1,0:T(8,128)(2,1)S(1)}, bf16[64,1024]{1,0:T(8,128)(2,1)S(1)}, u32[]{:S(2)}, u32[]{:S(2)}) collective-permute-start(bf16[64,1024]{1,0:T(8,128)(2,1)S(1)} %collective-permute-done.1.refs_2_), channel_id=1, source_target_pairs={{0,2},{2,0},{4,6},{6,4},{8,10},{10,8},{12,14},{14,12},{1,3},{3,1},... | collective-permute-start | bytes 393224 | tf_op jit(solution)/shard_map/ppermute | solution.py:172
  21.0 0.1 pad_add_fusion.cand_ref
  21.1 0.0 collective-permute-done.refs_1_
  21.1 1.7 %collective-permute-done.6.refs_7_ = bf16[64,1024]{1,0:T(8,128)(2,1)S(1)} collective-permute-done((bf16[64,1024]{1,0:T(8,128)(2,1)}, bf16[64,1024]{1,0:T(8,128)(2,1)S(1)}, u32[]{:S(2)}, u32[]{:S(2)}) %collective-permute-start.6) | collective-permute-done | bytes 131104 | tf_op jit(solution)/shard_map/ppermute | solution.py:172
  22.8 4.0 %collective-permute-done.2.refs_3_ = bf16[64,1024]{1,0:T(8,128)(2,1)S(1)} collective-permute-done((bf16[64,1024]{1,0:T(8,128)(2,1)S(1)}, bf16[64,1024]{1,0:T(8,128)(2,1)S(1)}, u32[]{:S(2)}, u32[]{:S(2)}) %collective-permute-start.2) | collective-permute-done | bytes 131104 | tf_op jit(solution)/shard_map/ppermute | solution.py:172
  26.8 0.0 collective-permute-done.4.refs_5_
  26.8 0.0 collective-permute-done.5.refs_6_
  26.8 0.0 copy-start.4
  26.8 2.2 %copy-done.4 = bf16[2048,1024]{1,0:T(8,128)(2,1)S(1)} copy-done((bf16[2048,1024]{1,0:T(8,128)(2,1)S(1)}, bf16[2048,1024]{1,0:T(8,128)(2,1)}, u32[]{:S(2)}) %copy-start.4) | copy-done | bytes 4194328
  29.0 0.0 copy-start.5
  29.0 0.9 %copy-done.5 = bf16[64,1024]{1,0:T(8,128)(2,1)S(1)} copy-done((bf16[64,1024]{1,0:T(8,128)(2,1)S(1)}, bf16[64,1024]{1,0:T(8,128)(2,1)}, u32[]{:S(2)}) %copy-start.5) | copy-done | bytes 131096
  29.9 3.2 %exact.1 = (f32[16,64]{1,0:T(8,128)S(1)}, f32[16,64]{1,0:T(8,128)S(1)}, f32[16,64]{1,0:T(8,128)S(1)}, f32[16,64]{1,0:T(8,128)S(1)}, f32[16,64]{1,0:T(8,128)S(1)}...) custom-call(s32[1]{0:T(128)} %bitcast.4.base_ref, s32[16,512]{1,0:T(8,128)S(1)} %pad_add_fusion.cand_ref, ...), custom_call_target="tpu_custom_call" | custom-call | flops 2147483648 | bytes 4194304 | tf_op jit(solution)/shard_map/exact/pallas_call | solution.py:108
  33.1 0.0 copy-start.8
  33.1 0.0 copy-start.6
  33.1 0.0 copy-start.7
  33.1 2.7 %collective-permute-start.16 = (f32[16,64]{1,0:T(8,128)S(1)}, f32[16,64]{1,0:T(8,128)S(1)}, u32[]{:S(2)}, u32[]{:S(2)}) collective-permute-start(f32[16,64]{1,0:T(8,128)S(1)} %get-tuple-element.17), channel_id=1, source_target_pairs={{0,14},{2,12},{4,10},{6,8},{8,6},{10,4},{12,2},{14,0},{1,15},{3,13... | collective-permute-start | bytes 12296 | tf_op jit(solution)/shard_map/ppermute | solution.py:172
  35.8 1.4 %collective-permute-start.15 = (f32[16,64]{1,0:T(8,128)S(1)}, f32[16,64]{1,0:T(8,128)S(1)}, u32[]{:S(2)}, u32[]{:S(2)}) collective-permute-start(f32[16,64]{1,0:T(8,128)S(1)} %get-tuple-element.16), channel_id=1, source_target_pairs={{0,12},{2,14},{4,8},{6,10},{8,4},{10,6},{12,0},{14,2},{1,13},{3,15... | collective-permute-start | bytes 12296 | tf_op jit(solution)/shard_map/ppermute | solution.py:172
  37.2 0.0 copy-done.2
  37.2 0.0 copy-done.3
  37.2 4.7 %decode.1.rows_ref = bf16[2048,1024]{1,0:T(8,128)(2,1)S(1)} custom-call(s32[2048,256]{1,0:T(8,128)S(1)} %copy-done.2, bf16[16,1024]{1,0:T(8,128)(2,1)S(1)} %copy-done.3), custom_call_target="tpu_custom_call" | custom-call | flops 1073741824 | bytes 8388608 | tf_op jit(solution)/shard_map/decode/pallas_call | solution.py:55
  41.9 0.0 copy-start
  41.9 1.9 %copy-done = bf16[2048,1024]{1,0:T(8,128)(2,1)} copy-done((bf16[2048,1024]{1,0:T(8,128)(2,1)}, bf16[2048,1024]{1,0:T(8,128)(2,1)S(1)}, u32[]{:S(2)}) %copy-start) | copy-done | bytes 4194328
  43.9 0.0 copy-done.8
  43.9 0.1 copy.10.ids_ref
  43.9 0.0 collective-permute-start.14
  43.9 3.6 %collective-permute-start.13 = (f32[16,64]{1,0:T(8,128)S(1)}, f32[16,64]{1,0:T(8,128)S(1)}, u32[]{:S(2)}, u32[]{:S(2)}) collective-permute-start(f32[16,64]{1,0:T(8,128)S(1)} %get-tuple-element.14), channel_id=1, source_target_pairs={{0,8},{2,10},{4,12},{6,14},{8,0},{10,2},{12,4},{14,6},{1,9},{3,11}... | collective-permute-start | bytes 12296 | tf_op jit(solution)/shard_map/ppermute | solution.py:172
  47.5 0.3 collective-permute-start.12
  47.9 0.0 collective-permute-done.16
  47.9 1.9 %collective-permute-start.11 = (f32[16,64]{1,0:T(8,128)S(1)}, f32[16,64]{1,0:T(8,128)S(1)}, u32[]{:S(2)}, u32[]{:S(2)}) collective-permute-start(f32[16,64]{1,0:T(8,128)S(1)} %get-tuple-element.12), channel_id=1, source_target_pairs={{0,4},{2,6},{4,0},{6,2},{8,12},{10,14},{12,8},{14,10},{1,5},{3,7},... | collective-permute-start | bytes 12296 | tf_op jit(solution)/shard_map/ppermute | solution.py:172
  49.8 0.0 collective-permute-done.15
  49.8 1.3 %collective-permute-start.10 = (f32[16,64]{1,0:T(8,128)S(1)}, f32[16,64]{1,0:T(8,128)S(1)}, u32[]{:S(2)}, u32[]{:S(2)}) collective-permute-start(f32[16,64]{1,0:T(8,128)S(1)} %get-tuple-element.11), channel_id=1, source_target_pairs={{0,2},{2,0},{4,6},{6,4},{8,10},{10,8},{12,14},{14,12},{1,3},{3,1},... | collective-permute-start | bytes 12296 | tf_op jit(solution)/shard_map/ppermute | solution.py:172
  51.0 0.0 copy-done.6
  51.0 0.0 copy-done.7
  51.1 0.0 copy-start.1
  51.1 2.2 %copy-done.1 = bf16[2048,1024]{1,0:T(8,128)(2,1)S(1)} copy-done((bf16[2048,1024]{1,0:T(8,128)(2,1)S(1)}, bf16[2048,1024]{1,0:T(8,128)(2,1)}, u32[]{:S(2)}) %copy-start.1) | copy-done | bytes 4194328
  53.2 4.1 %approx.1 = bf16[8,4,64,256]{3,2,1,0:T(8,128)(2,1)} custom-call(s32[8]{0:T(128)S(1)} %iota_xor_fusion.where_ref, s32[8,4]{1,0:T(8,128)S(1)} %copy.10.ids_ref, s32[8]{0:T(128)S(1)} %bitcast.12, bf16[2048,1024]{1,0:T(8,128)(2,1)S(1)} %copy-done.1, bf16[64,1024]{1,0:T(8,128)(2,1)S(1)} %copy-done.6, bf16[64,1024]{1,0:T(8,128)(2,1)S(1)} %collective-permute-done.refs_1_, ...), custom_call_target="tpu_custom_call" | custom-call | flops 2147483648 | bytes 4194304 | tf_op jit(solution)/shard_map/approx/pallas_call | solution.py:152
  57.3 0.0 collective-permute-done.14
  57.3 0.0 collective-permute-done.13
  57.3 0.0 collective-permute-done.12
  57.3 0.0 collective-permute-done.11
  57.3 0.0 collective-permute-done.10
  57.3 0.6 %add_add_fusion = f32[16,64]{1,0:T(8,128)} fusion(f32[16,64]{1,0:T(8,128)S(1)} %collective-permute-done.16, f32[16,64]{1,0:T(8,128)S(1)} %collective-permute-done.15, f32[16,64]{1,0:T(8,128)S(1)} %collective-permute-done.14, f32[16,64]{1,0:T(8,128)S(1)} %collective-permute-done.13, f32[16,64]{1,0:T(8,128)S(1)} %collective-permute-done.12, ...), kind=kLoop, calls=%fused_computation.3 | loop fusion | flops 7168 | bytes 36864 | tf_op jit(solution)/shard_map/add | solution.py:205
  (1 shorter events, 0.0 us)
Async XLA Ops:
  0.6 36.6 %copy-start.2 = (s32[2048,256]{1,0:T(8,128)S(1)}, s32[2048,256]{1,0:T(8,128)}, u32[]{:S(2)}) copy-start(s32[2048,256]{1,0:T(8,128)} %codes_ref.1) | copy-start | bytes 6291460
  0.6 36.6 %copy-start.3 = (bf16[16,1024]{1,0:T(8,128)(2,1)S(1)}, bf16[16,1024]{1,0:T(8,128)(2,1)}, u32[]{:S(2)}) copy-start(bf16[16,1024]{1,0:T(8,128)(2,1)} %book_ref.1) | copy-start | bytes 98308
  1.5 4.6 %collective-permute-start.7 = (s32[16,64]{1,0:T(8,128)S(1)}, s32[16,64]{1,0:T(8,128)S(1)}, u32[]{:S(2)}, u32[]{:S(2)}) collective-permute-start(s32[16,64]{1,0:T(8,128)S(1)} %bitcast.13), channel_id=1, source_target_pairs={{0,2},{2,0},{4,6},{6,4},{8,10},{10,8},{12,14},{14,12},{1,3},{3,1},... | collective-permute-start | bytes 12296 | tf_op jit(solution)/shard_map/ppermute | solution.py:172
  6.2 5.1 %collective-permute-start.8 = (s32[16,128]{1,0:T(8,128)S(1)}, s32[16,128]{1,0:T(8,128)S(1)}, u32[]{:S(2)}, u32[]{:S(2)}) collective-permute-start(s32[16,128]{1,0:T(8,128)S(1)} %pad_add_fusion.2), channel_id=1, source_target_pairs={{0,4},{2,6},{4,0},{6,2},{8,12},{10,14},{12,8},{14,10},{1,5},{3,7},... | collective-permute-start | bytes 24584 | tf_op jit(solution)/shard_map/ppermute | solution.py:172
  8.3 10.3 %collective-permute-start.3 = (bf16[64,1024]{1,0:T(8,128)(2,1)}, bf16[64,1024]{1,0:T(8,128)(2,1)S(1)}, u32[]{:S(2)}, u32[]{:S(2)}) collective-permute-start(bf16[64,1024]{1,0:T(8,128)(2,1)} %refs_0_.3), channel_id=1, source_target_pairs={{0,8},{2,10},{4,12},{6,14},{8,0},{10,2},{12,4},{14,6},{1,9},{3,11}... | collective-permute-start | bytes 393224 | tf_op jit(solution)/shard_map/ppermute | solution.py:172
  10.9 9.4 %collective-permute-start.1 = (bf16[64,1024]{1,0:T(8,128)(2,1)}, bf16[64,1024]{1,0:T(8,128)(2,1)S(1)}, u32[]{:S(2)}, u32[]{:S(2)}) collective-permute-start(bf16[64,1024]{1,0:T(8,128)(2,1)} %refs_0_.3), channel_id=1, source_target_pairs={{0,4},{2,6},{4,0},{6,2},{8,12},{10,14},{12,8},{14,10},{1,5},{3,7},... | collective-permute-start | bytes 393224 | tf_op jit(solution)/shard_map/ppermute | solution.py:172
  11.4 8.8 %collective-permute-start.9 = (s32[16,256]{1,0:T(8,128)S(1)}, s32[16,256]{1,0:T(8,128)S(1)}, u32[]{:S(2)}, u32[]{:S(2)}) collective-permute-start(s32[16,256]{1,0:T(8,128)S(1)} %pad_add_fusion.1), channel_id=1, source_target_pairs={{0,8},{2,10},{4,12},{6,14},{8,0},{10,2},{12,4},{14,6},{1,9},{3,11}... | collective-permute-start | bytes 49160 | tf_op jit(solution)/shard_map/ppermute | solution.py:172
  13.2 7.9 %collective-permute-start = (bf16[64,1024]{1,0:T(8,128)(2,1)}, bf16[64,1024]{1,0:T(8,128)(2,1)S(1)}, u32[]{:S(2)}, u32[]{:S(2)}) collective-permute-start(bf16[64,1024]{1,0:T(8,128)(2,1)} %refs_0_.3), channel_id=1, source_target_pairs={{0,2},{2,0},{4,6},{6,4},{8,10},{10,8},{12,14},{14,12},{1,3},{3,1},... | collective-permute-start | bytes 393224 | tf_op jit(solution)/shard_map/ppermute | solution.py:172
  14.7 8.1 %collective-permute-start.6 = (bf16[64,1024]{1,0:T(8,128)(2,1)}, bf16[64,1024]{1,0:T(8,128)(2,1)S(1)}, u32[]{:S(2)}, u32[]{:S(2)}) collective-permute-start(bf16[64,1024]{1,0:T(8,128)(2,1)} %refs_0_.3), channel_id=1, source_target_pairs={{0,14},{2,12},{4,10},{6,8},{8,6},{10,4},{12,2},{14,0},{1,15},{3,13... | collective-permute-start | bytes 393224 | tf_op jit(solution)/shard_map/ppermute | solution.py:172
  18.6 8.2 %collective-permute-start.4 = (bf16[64,1024]{1,0:T(8,128)(2,1)S(1)}, bf16[64,1024]{1,0:T(8,128)(2,1)S(1)}, u32[]{:S(2)}, u32[]{:S(2)}) collective-permute-start(bf16[64,1024]{1,0:T(8,128)(2,1)S(1)} %collective-permute-done.3.refs_4_), channel_id=1, source_target_pairs={{0,2},{2,0},{4,6},{6,4},{8,10},{10,8},{12,14},{14,12},{1,3},{3,1},... | collective-permute-start | bytes 393224 | tf_op jit(solution)/shard_map/ppermute | solution.py:172
  20.2 6.5 %collective-permute-start.5 = (bf16[64,1024]{1,0:T(8,128)(2,1)S(1)}, bf16[64,1024]{1,0:T(8,128)(2,1)S(1)}, u32[]{:S(2)}, u32[]{:S(2)}) collective-permute-start(bf16[64,1024]{1,0:T(8,128)(2,1)S(1)} %collective-permute-done.3.refs_4_), channel_id=1, source_target_pairs={{0,4},{2,6},{4,0},{6,2},{8,12},{10,14},{12,8},{14,10},{1,5},{3,7},... | collective-permute-start | bytes 393224 | tf_op jit(solution)/shard_map/ppermute | solution.py:172
  20.2 6.5 %collective-permute-start.2 = (bf16[64,1024]{1,0:T(8,128)(2,1)S(1)}, bf16[64,1024]{1,0:T(8,128)(2,1)S(1)}, u32[]{:S(2)}, u32[]{:S(2)}) collective-permute-start(bf16[64,1024]{1,0:T(8,128)(2,1)S(1)} %collective-permute-done.1.refs_2_), channel_id=1, source_target_pairs={{0,2},{2,0},{4,6},{6,4},{8,10},{10,8},{12,14},{14,12},{1,3},{3,1},... | collective-permute-start | bytes 393224 | tf_op jit(solution)/shard_map/ppermute | solution.py:172
  26.8 2.2 %copy-start.4 = (bf16[2048,1024]{1,0:T(8,128)(2,1)S(1)}, bf16[2048,1024]{1,0:T(8,128)(2,1)}, u32[]{:S(2)}) copy-start(bf16[2048,1024]{1,0:T(8,128)(2,1)} %rows_ref.1) | copy-start | bytes 12582916
  29.0 0.9 %copy-start.5 = (bf16[64,1024]{1,0:T(8,128)(2,1)S(1)}, bf16[64,1024]{1,0:T(8,128)(2,1)}, u32[]{:S(2)}) copy-start(bf16[64,1024]{1,0:T(8,128)(2,1)} %refs_0_.3) | copy-start | bytes 393220
  33.1 10.8 %copy-start.8 = (s32[8,1,1,4]{0,3,2,1:T(4,128)S(1)}, s32[8,1,1,4]{0,3,2,1:T(4,128)}, u32[]{:S(2)}) copy-start(s32[8,1,1,4]{0,3,2,1:T(4,128)} %param.12) | copy-start | bytes 388
  33.1 17.9 %copy-start.6 = (bf16[64,1024]{1,0:T(8,128)(2,1)S(1)}, bf16[64,1024]{1,0:T(8,128)(2,1)}, u32[]{:S(2)}) copy-start(bf16[64,1024]{1,0:T(8,128)(2,1)} %refs_0_.3) | copy-start | bytes 393220
  33.1 17.9 %copy-start.7 = (s32[8,1,1]{0,2,1:T(1,128)S(1)}, s32[8,1,1]{0,2,1:T(1,128)}, u32[]{:S(2)}) copy-start(s32[8,1,1]{0,2,1:T(1,128)} %param.13) | copy-start | bytes 100
  33.1 14.7 %collective-permute-start.16 = (f32[16,64]{1,0:T(8,128)S(1)}, f32[16,64]{1,0:T(8,128)S(1)}, u32[]{:S(2)}, u32[]{:S(2)}) collective-permute-start(f32[16,64]{1,0:T(8,128)S(1)} %get-tuple-element.17), channel_id=1, source_target_pairs={{0,14},{2,12},{4,10},{6,8},{8,6},{10,4},{12,2},{14,0},{1,15},{3,13... | collective-permute-start | bytes 12296 | tf_op jit(solution)/shard_map/ppermute | solution.py:172
  35.8 13.9 %collective-permute-start.15 = (f32[16,64]{1,0:T(8,128)S(1)}, f32[16,64]{1,0:T(8,128)S(1)}, u32[]{:S(2)}, u32[]{:S(2)}) collective-permute-start(f32[16,64]{1,0:T(8,128)S(1)} %get-tuple-element.16), channel_id=1, source_target_pairs={{0,12},{2,14},{4,8},{6,10},{8,4},{10,6},{12,0},{14,2},{1,13},{3,15... | collective-permute-start | bytes 12296 | tf_op jit(solution)/shard_map/ppermute | solution.py:172
  41.9 1.9 %copy-start = (bf16[2048,1024]{1,0:T(8,128)(2,1)}, bf16[2048,1024]{1,0:T(8,128)(2,1)S(1)}, u32[]{:S(2)}) copy-start(bf16[2048,1024]{1,0:T(8,128)(2,1)S(1)} %decode.1.rows_ref) | copy-start | bytes 12582916
  43.9 13.4 %collective-permute-start.14 = (f32[16,64]{1,0:T(8,128)S(1)}, f32[16,64]{1,0:T(8,128)S(1)}, u32[]{:S(2)}, u32[]{:S(2)}) collective-permute-start(f32[16,64]{1,0:T(8,128)S(1)} %get-tuple-element.15), channel_id=1, source_target_pairs={{0,10},{2,8},{4,14},{6,12},{8,2},{10,0},{12,6},{14,4},{1,11},{3,9}... | collective-permute-start | bytes 12296 | tf_op jit(solution)/shard_map/ppermute | solution.py:172
  43.9 13.4 %collective-permute-start.13 = (f32[16,64]{1,0:T(8,128)S(1)}, f32[16,64]{1,0:T(8,128)S(1)}, u32[]{:S(2)}, u32[]{:S(2)}) collective-permute-start(f32[16,64]{1,0:T(8,128)S(1)} %get-tuple-element.14), channel_id=1, source_target_pairs={{0,8},{2,10},{4,12},{6,14},{8,0},{10,2},{12,4},{14,6},{1,9},{3,11}... | collective-permute-start | bytes 12296 | tf_op jit(solution)/shard_map/ppermute | solution.py:172
  47.5 9.8 %collective-permute-start.12 = (f32[16,64]{1,0:T(8,128)S(1)}, f32[16,64]{1,0:T(8,128)S(1)}, u32[]{:S(2)}, u32[]{:S(2)}) collective-permute-start(f32[16,64]{1,0:T(8,128)S(1)} %get-tuple-element.13), channel_id=1, source_target_pairs={{0,6},{2,4},{4,2},{6,0},{8,14},{10,12},{12,10},{14,8},{1,7},{3,5},... | collective-permute-start | bytes 12296 | tf_op jit(solution)/shard_map/ppermute | solution.py:172
  47.9 9.5 %collective-permute-start.11 = (f32[16,64]{1,0:T(8,128)S(1)}, f32[16,64]{1,0:T(8,128)S(1)}, u32[]{:S(2)}, u32[]{:S(2)}) collective-permute-start(f32[16,64]{1,0:T(8,128)S(1)} %get-tuple-element.12), channel_id=1, source_target_pairs={{0,4},{2,6},{4,0},{6,2},{8,12},{10,14},{12,8},{14,10},{1,5},{3,7},... | collective-permute-start | bytes 12296 | tf_op jit(solution)/shard_map/ppermute | solution.py:172
  49.8 7.5 %collective-permute-start.10 = (f32[16,64]{1,0:T(8,128)S(1)}, f32[16,64]{1,0:T(8,128)S(1)}, u32[]{:S(2)}, u32[]{:S(2)}) collective-permute-start(f32[16,64]{1,0:T(8,128)S(1)} %get-tuple-element.11), channel_id=1, source_target_pairs={{0,2},{2,0},{4,6},{6,4},{8,10},{10,8},{12,14},{14,12},{1,3},{3,1},... | collective-permute-start | bytes 12296 | tf_op jit(solution)/shard_map/ppermute | solution.py:172
  51.1 2.2 %copy-start.1 = (bf16[2048,1024]{1,0:T(8,128)(2,1)S(1)}, bf16[2048,1024]{1,0:T(8,128)(2,1)}, u32[]{:S(2)}) copy-start(bf16[2048,1024]{1,0:T(8,128)(2,1)} %copy-done) | copy-start | bytes 12582916

commit v2 on v1

v2 whole, which is shorter than its diff:
```python
import functools

import jax
import jax.numpy as jnp
from jax import lax
from jax.experimental import pallas as pl
from jax.experimental.pallas import tpu as pltpu
from jax.sharding import PartitionSpec as P

B = 256
NT = (((1,), (1,)), ((), ()))
IN_VMEM = pl.BlockSpec(memory_space=pltpu.VMEM)
IN_HBM = pl.BlockSpec(memory_space=pl.ANY)
IN_SMEM = pl.BlockSpec(memory_space=pltpu.SMEM)
LIMIT = 24 * 2**20


def params():
    return pltpu.CompilerParams(vmem_limit_bytes=LIMIT)


def pick(table, index):
    return jnp.take_along_axis(table, index, axis=0, mode="promise_in_bounds")


def regroup_matrix(sub_width):
    run = 256 // sub_width
    source = lax.broadcasted_iota(jnp.int32, (256, 256), 0)
    target = lax.broadcasted_iota(jnp.int32, (256, 256), 1)
    return (source == (target % run) * sub_width + target // run).astype(jnp.bfloat16)


def decode_kernel(
    queries_ref, codes_ref, book_ref, rows_ref, shard_ref, row_ref,
    out_ref, rows_out, queries_out, wanted_out,
    codes, book, tables, shard, row, code_sems, row_sems, small_sems,
    *, step,
):
    row_count, code_count = codes_ref.shape
    features = book_ref.shape[1]
    sub_width = features // code_count
    parts = row_count // step
    small = [
        pltpu.make_async_copy(source, target, small_sems.at[at])
        for at, (source, target) in enumerate(
            [(book_ref, book), (shard_ref, shard), (row_ref, row), (queries_ref, queries_out)]
        )
    ]
    for copy in small:
        copy.start()
    for part in range(parts):
        here = pl.ds(part * step, step)
        pltpu.make_async_copy(codes_ref.at[here], codes.at[here], code_sems.at[part]).start()
    row_copies = []
    for part in range(4):
        here = pl.ds(part * (row_count // 4), row_count // 4)
        row_copies.append(
            pltpu.make_async_copy(rows_ref.at[here], rows_out.at[here], row_sems.at[part])
        )
        row_copies[-1].start()
    regroup = regroup_matrix(sub_width)
    small[0].wait()
    for left in range(0, features, 256):
        tables[:, left : left + 256] = jnp.dot(
            book[:, left : left + 256], regroup, preferred_element_type=jnp.float32
        )

    @pl.loop(0, parts)
    def _(at):
        start = pl.multiple_of(at * step, step)
        here = pl.ds(start, step)
        pltpu.make_async_copy(codes_ref.at[here], codes.at[here], code_sems.at[at]).wait()
        first = lax.broadcasted_iota(jnp.int32, (step, 128), 1) < 64
        for pair in range(code_count // 128):
            both = codes[here, pair * 128 : (pair + 1) * 128]
            turned = pltpu.roll(both, 64, 1)
            for side in range(2):
                index = jnp.where(first, both, turned) if side == 0 else jnp.where(first, turned, both)
                inner = index & 7
                upper = index >= 8
                for half in range(2):
                    left = (pair * 2 + side) * 256 + half * 128
                    low = tables[:8, left : left + 128]
                    high = tables[8:16, left : left + 128]
                    pieces = []
                    for top in range(0, step, 8):
                        near = slice(top, top + 8)
                        pieces.append(
                            jnp.where(upper[near], pick(high, inner[near]), pick(low, inner[near]))
                        )
                    out_ref[here, left : left + 128] = jnp.concatenate(pieces, axis=0).astype(
                        jnp.bfloat16
                    )

    for copy in small[1:]:
        copy.wait()
    wanted_out[...] = shard[...] * row_count + row[...]
    for copy in row_copies:
        copy.wait()


def decode(queries, pq_codes, codebook, full_rows, cand_shard, cand_row):
    rows, code_count = pq_codes.shape
    features = codebook.shape[1]
    step = 256
    return pl.pallas_call(
        functools.partial(decode_kernel, step=step),
        out_shape=[
            pltpu.VMEM((rows, features), jnp.bfloat16),
            pltpu.VMEM(full_rows.shape, full_rows.dtype),
            pltpu.VMEM(queries.shape, queries.dtype),
            pltpu.VMEM(cand_row.shape, jnp.int32),
        ],
        in_specs=[IN_HBM] * 6,
        out_specs=[IN_VMEM] * 4,
        scratch_shapes=[
            pltpu.VMEM(pq_codes.shape, jnp.int32),
            pltpu.VMEM(codebook.shape, codebook.dtype),
            pltpu.VMEM(codebook.shape, jnp.float32),
            pltpu.VMEM(cand_row.shape, jnp.int32),
            pltpu.VMEM(cand_row.shape, jnp.int32),
            pltpu.SemaphoreType.DMA((rows // step,)),
            pltpu.SemaphoreType.DMA((4,)),
            pltpu.SemaphoreType.DMA((4,)),
        ],
        compiler_params=params(),
        cost_estimate=pl.CostEstimate(
            flops=2 * rows * code_count * features, bytes_accessed=8 * 2**20, transcendentals=0
        ),
        name="decode",
    )(*map(in_hbm, (queries, pq_codes, codebook, full_rows, cand_shard, cand_row)))


def in_hbm(x):
    return pltpu.with_memory_space_constraint(x, pltpu.HBM)


def in_vmem(x):
    return pltpu.with_memory_space_constraint(x, pltpu.VMEM)


def exact_kernel(cand_ref, rows_ref, *refs, groups):
    blocks, out_ref, stack = refs[:-2], refs[-2], refs[-1]
    query_rows = blocks[0].shape[0]
    row_count = rows_ref.shape[0]
    per_query, width = cand_ref.shape
    tops = per_query // groups
    for at, block in enumerate(blocks):
        stack[at * query_rows : (at + 1) * query_rows, :] = block[...]
    scores = lax.dot_general(
        rows_ref[...], stack[...], NT, preferred_element_type=jnp.float32
    )
    wanted = cand_ref[...] - lax.axis_index("corpus") * row_count
    mine = (wanted >= 0) & (wanted < row_count)
    kept = jnp.where(mine, wanted, -1)
    down = lax.broadcasted_iota(jnp.int32, (8, width), 0)
    found = []
    for group in range(groups):
        row = jnp.max(kept[group * tops : (group + 1) * tops], axis=0, keepdims=True)
        row = jnp.broadcast_to(row, (8, width)) - down
        total = jnp.zeros((8, width), jnp.float32)
        for top in range(0, row_count, 8):
            total = jnp.where(row == top, scores[top : top + 8], total)
        total = jnp.sum(total, axis=0, keepdims=True)
        found.append(jnp.broadcast_to(total, (tops, width)))
    out_ref[...] = jnp.where(mine, jnp.concatenate(found, axis=0), 0.0)


def exact(cands, full_rows, blocks, groups):
    query_rows, features = blocks[0].shape
    count = len(blocks)
    return pl.pallas_call(
        functools.partial(exact_kernel, groups=groups),
        out_shape=jax.ShapeDtypeStruct(cands.shape, jnp.float32),
        in_specs=[IN_VMEM] * (2 + count),
        out_specs=IN_VMEM,
        scratch_shapes=[pltpu.VMEM((count * query_rows, features), jnp.bfloat16)],
        compiler_params=params(),
        cost_estimate=pl.CostEstimate(
            flops=2 * count * query_rows * features * full_rows.shape[0],
            bytes_accessed=4 * 2**20,
            transcendentals=0,
        ),
        name="exact",
    )(cands, in_vmem(full_rows), *map(in_vmem, blocks))


def scores_kernel(rows_ref, *refs, sub_width):
    blocks, out_ref, stack = refs[:-2], refs[-2], refs[-1]
    query_rows, features = blocks[0].shape
    regroup = regroup_matrix(sub_width)
    for at, block in enumerate(blocks):
        stack[at * query_rows : (at + 1) * query_rows, :] = block[...]
    for left in range(0, features, 256):
        run = slice(left, left + 256)
        stack[:, run] = jnp.dot(
            stack[:, run], regroup, preferred_element_type=jnp.float32
        ).astype(jnp.bfloat16)
    for block in range(out_ref.shape[0]):
        out_ref[block] = lax.dot_general(
            stack[...],
            rows_ref[block * B : (block + 1) * B, :],
            NT,
            preferred_element_type=jnp.float32,
        ).astype(jnp.bfloat16)


def score_blocks(decoded, blocks, sub_width):
    query_rows, features = blocks[0].shape
    width = len(blocks) * query_rows
    block_count = decoded.shape[0] // B
    return pl.pallas_call(
        functools.partial(scores_kernel, sub_width=sub_width),
        out_shape=pltpu.VMEM((block_count, width, B), jnp.bfloat16),
        in_specs=[IN_VMEM] * (1 + len(blocks)),
        out_specs=IN_VMEM,
        scratch_shapes=[pltpu.VMEM((width, features), jnp.bfloat16)],
        compiler_params=params(),
        cost_estimate=pl.CostEstimate(
            flops=2 * width * features * decoded.shape[0],
            bytes_accessed=4 * 2**20,
            transcendentals=0,
        ),
        name="score_blocks",
    )(in_vmem(decoded), *map(in_vmem, blocks))


def choose_kernel(ids_ref, len_ref, scores_ref, out_ref, *, mirrored):
    count, slots, query_rows, _ = out_ref.shape
    for at in range(count):
        owner = lax.axis_index("corpus") ^ at if mirrored else at
        here = slice(at * query_rows, (at + 1) * query_rows)
        for slot in range(slots):
            picked = scores_ref[ids_ref[slot, owner], here, :]
            out_ref[owner, slot] = jnp.where(slot < len_ref[owner], picked, jnp.zeros_like(picked))


def choose(probe_ids, probe_len, scores, mirrored):
    slots, count = probe_ids.shape
    query_rows = scores.shape[1] // count
    return pl.pallas_call(
        functools.partial(choose_kernel, mirrored=mirrored),
        out_shape=jax.ShapeDtypeStruct((count, slots, query_rows, B), jnp.bfloat16),
        in_specs=[IN_SMEM] * 2 + [IN_VMEM],
        out_specs=IN_VMEM,
        compiler_params=params(),
        cost_estimate=pl.CostEstimate(flops=0, bytes_accessed=4 * 2**20, transcendentals=0),
        name="choose",
    )(probe_ids, probe_len, in_vmem(scores))


def swap(x, distance, shards):
    return lax.ppermute(x, "corpus", [(i, i ^ distance) for i in range(shards)])


def local(queries, codebook, pq_codes, full_rows, probe_ids, probe_len, cand_shard, cand_row):
    shards = lax.axis_size("corpus")
    query_rows, features = queries.shape
    groups, tops = cand_shard.shape[1:]
    per_query = groups * tops
    slots = probe_ids.shape[-1]
    sub_width = features // pq_codes.shape[1]
    ids = probe_ids.reshape(shards, slots).T
    lens = probe_len.reshape(shards)
    prepare = functools.partial(
        decode,
        queries,
        pq_codes,
        codebook,
        full_rows,
        cand_shard.reshape(query_rows, per_query).T,
        cand_row.reshape(query_rows, per_query).T,
    )

    if shards == 8:
        far = swap(queries, 4, shards)
        near = swap(queries, 2, shards)
        side = swap(queries, 1, shards)
        decoded, rows, own, wanted = prepare()
        cross = swap(own, 7, shards)
        near_side = swap(near, 1, shards)
        far_near = swap(far, 2, shards)
        far_side = swap(far, 1, shards)
        for distance in (1, 2):
            wanted = jnp.concatenate([wanted, swap(wanted, distance, shards)], axis=1)
        wanted_far = swap(wanted, 4, shards)
        this_half = [own, side, near, near_side]
        that_half = [far, far_side, far_near, cross]
        kept = exact(wanted, rows, this_half, groups)
        sent = exact(wanted_far, rows, that_half, groups)
        scores = score_blocks(decoded, this_half + that_half, sub_width)
        approx_scores = choose(ids, lens, scores, True)
        for distance in (4, 2, 1):
            kept = kept + swap(sent, distance, shards)
            half = kept.shape[1] // 2
            kept, sent = kept[:, :half], kept[:, half:]
        total = jnp.concatenate([kept, sent], axis=1)
    else:
        gathered = lax.all_gather(queries, "corpus", axis=0)
        decoded, rows, _, wanted = prepare()
        asked = lax.all_gather(wanted, "corpus", axis=0)
        answers, pieces = [], []
        step = 4
        for first in range(0, shards, step):
            picked = list(range(first, first + step))
            blocks = [gathered[p] for p in picked]
            cands = jnp.concatenate([asked[p] for p in picked], axis=1)
            found = exact(cands, rows, blocks, groups)
            answers += [found[:, p * query_rows : (p + 1) * query_rows] for p in range(step)]
            scores = score_blocks(decoded, blocks, sub_width)
            some = slice(first, first + step)
            pieces.append(choose(ids[:, some], lens[some], scores, False))
        approx_scores = jnp.concatenate(pieces, axis=0)
        back = lax.all_to_all(jnp.stack(answers), "corpus", 0, 0, tiled=True)
        total = jnp.sum(back, axis=0)

    approx_scores = approx_scores.reshape(shards, 1, 1, slots, query_rows, B)
    return approx_scores, total.T.reshape(query_rows, groups, tops)


def solution(mesh):
    return jax.shard_map(
        local,
        mesh=mesh,
        in_specs=(
            P(("groups", "corpus", "replica"), None),
            P("groups", None),
            P(("groups", "corpus"), None),
            P(("groups", "corpus"), None),
            P("groups", "replica", "corpus", None),
            P("groups", "replica", "corpus"),
            P(("groups", "corpus", "replica"), None, None),
            P(("groups", "corpus", "replica"), None, None),
        ),
        out_specs=(
            P("groups", "replica", "corpus", None, None, None),
            P(("groups", "corpus", "replica"), None, None),
        ),
        check_vma=False,
    )
```

time: 58.2 us -> 41.6 us (0.71)
  local copies, waits for them, and re-layouts: 7.31 us -> 0.1 us
  starting transfers between devices: 27.1 us -> 21.1 us
  waiting for transfers between devices: 9.14 us -> 7.39 us
  other arithmetic: 1.7 us -> 0.76 us
  Pallas kernels: 12 us -> 11.4 us
    unnamed x18 -> x6, local copies, waits for them, and re-layouts: 7.23 us -> 0.02 us
    ppermute x17 -> x13, starting transfers between devices: 27.1 us -> 21.1 us  [swap(): return lax.ppermute(x, 'corpus', [(i, i ^ distance) for i in range(shards)])]
    ppermute x17 -> x13, waiting for transfers between devices: 9.14 us -> 7.39 us  [swap(): return lax.ppermute(x, 'corpus', [(i, i ^ distance) for i in range(shards)])]
    add x2 -> x3, other arithmetic: 1.48 us -> 0.61 us  [local(): kept = kept + swap(sent, distance, shards)]
    pallas_call x3 -> x5, Pallas kernels: 12 us -> 11.4 us  [the longest x1 4.01 us: decode(): pl.pallas_call(functools.partial(decode_kernel, step=step), out_shape=[pl...]
  transfers between devices with their start and end apart: 17 -> 13, of which waited for: 4 -> 5; matrix products, arithmetic and copies ran while one was open for 0% -> 0% of each run, Pallas kernels for 15% -> 27%
where the time goes in v2:
time: 41.6 us; the launch traced here: 41.5 us
  starting transfers between devices  21.1 us (51%)
  Pallas kernels  11.4 us (27%)
  waiting for transfers between devices  7.39 us (18%)
  other arithmetic  0.76 us (2%)
  between operations  0.72 us (2%)
    ppermute x13, starting transfers between devices, swap(): return lax.ppermute(x, 'corpus', [(i, i ^ distance) for i in range(shards)])  21.1 us
    ppermute x13, waiting for transfers between devices, swap(): return lax.ppermute(x, 'corpus', [(i, i ^ distance) for i in range(shards)])  7.39 us
    pallas_call x1, Pallas kernels, decode(): pl.pallas_call(functools.partial(decode_kernel, step=step), out_shape=[pl...  4.01 us
    pallas_call x2, Pallas kernels, exact(): pl.pallas_call(functools.partial(exact_kernel, groups=groups), out_shape=...  3.02 us
    pallas_call x1, Pallas kernels, score_blocks(): pl.pallas_call(functools.partial(scores_kernel, sub_width=sub_width), out...  2.61 us
    pallas_call x1, Pallas kernels, choose(): pl.pallas_call(functools.partial(choose_kernel, mirrored=mirrored), out_s...  1.76 us
  transfers between devices with their start and end apart: 13, of which 5 were waited for; matrix products, arithmetic and copies ran while one was open for 0% of the time, Pallas kernels for 27%

profile of v2, /device:TPU:0, one launch (start us, length us, event | category | flops | bytes accessed | tf_op | source)
XLA Modules:
  0.0 41.5 jit_solution(16903458104395501387)
XLA Ops:
  0.6 0.0 copy-start.2
  0.6 4.1 %collective-permute-start.3 = (bf16[64,1024]{1,0:T(8,128)(2,1)}, bf16[64,1024]{1,0:T(8,128)(2,1)S(1)}, u32[]{:S(2)}, u32[]{:S(2)}) collective-permute-start(bf16[64,1024]{1,0:T(8,128)(2,1)} %queries_ref.1), channel_id=1, source_target_pairs={{0,8},{2,10},{4,12},{6,14},{8,0},{10,2},{12,4},{14,6},{1,9},{3,11}... | collective-permute-start | bytes 393224 | tf_op jit(solution)/shard_map/ppermute | solution.py:253
  4.7 4.0 %decode.1 = (bf16[2048,1024]{1,0:T(8,128)(2,1)S(1)}, bf16[2048,1024]{1,0:T(8,128)(2,1)S(1)}, bf16[64,1024]{1,0:T(8,128)(2,1)S(1)}, s32[16,64]{1,0:T(8,128)S(1)}) custom-call(bf16[64,1024]{1,0:T(8,128)(2,1)} %queries_ref.1, s32[2048,256]{1,0:T(8,128)} %codes_ref.1, bf16[16,1024]{1,0:T(8,128)(2,1)} %book_ref.1, bf16[2048,1024]{1,0:T(8,128)(2,1)} %rows_ref.1, ...), custom_call_target="tpu_custom_call" | custom-call | flops 1073741824 | bytes 8388608 | tf_op jit(solution)/shard_map/decode/pallas_call | solution.py:106
  8.8 1.6 %collective-permute-start.7 = (s32[16,64]{1,0:T(8,128)S(1)}, s32[16,64]{1,0:T(8,128)S(1)}, u32[]{:S(2)}, u32[]{:S(2)}) collective-permute-start(s32[16,64]{1,0:T(8,128)S(1)} %get-tuple-element.8), channel_id=1, source_target_pairs={{0,2},{2,0},{4,6},{6,4},{8,10},{10,8},{12,14},{14,12},{1,3},{3,1},... | collective-permute-start | bytes 12296 | tf_op jit(solution)/shard_map/ppermute | solution.py:253
  10.3 2.1 %collective-permute-done.7 = s32[16,64]{1,0:T(8,128)S(1)} collective-permute-done((s32[16,64]{1,0:T(8,128)S(1)}, s32[16,64]{1,0:T(8,128)S(1)}, u32[]{:S(2)}, u32[]{:S(2)}) %collective-permute-start.7) | collective-permute-done | bytes 4128 | tf_op jit(solution)/shard_map/ppermute | solution.py:253
  12.5 0.1 pad_add_fusion.1
  12.6 1.6 %collective-permute-start.8 = (s32[16,128]{1,0:T(8,128)S(1)}, s32[16,128]{1,0:T(8,128)S(1)}, u32[]{:S(2)}, u32[]{:S(2)}) collective-permute-start(s32[16,128]{1,0:T(8,128)S(1)} %pad_add_fusion.1), channel_id=1, source_target_pairs={{0,4},{2,6},{4,0},{6,2},{8,12},{10,14},{12,8},{14,10},{1,5},{3,7},... | collective-permute-start | bytes 24584 | tf_op jit(solution)/shard_map/ppermute | solution.py:253
  14.1 0.0 copy-done.2
  14.1 0.4 %collective-permute-start.1 = (bf16[64,1024]{1,0:T(8,128)(2,1)S(1)}, bf16[64,1024]{1,0:T(8,128)(2,1)S(1)}, u32[]{:S(2)}, u32[]{:S(2)}) collective-permute-start(bf16[64,1024]{1,0:T(8,128)(2,1)S(1)} %copy-done.2), channel_id=1, source_target_pairs={{0,4},{2,6},{4,0},{6,2},{8,12},{10,14},{12,8},{14,10},{1,5},{3,7},... | collective-permute-start | bytes 393224 | tf_op jit(solution)/shard_map/ppermute | solution.py:253
  14.6 2.3 %collective-permute-start.6 = (bf16[64,1024]{1,0:T(8,128)(2,1)S(1)}, bf16[64,1024]{1,0:T(8,128)(2,1)S(1)}, u32[]{:S(2)}, u32[]{:S(2)}) collective-permute-start(bf16[64,1024]{1,0:T(8,128)(2,1)S(1)} %get-tuple-element.7.refs_0_), channel_id=1, source_target_pairs={{0,14},{2,12},{4,10},{6,8},{8,6},{10,4},{12,2},{14,0},{1,15},{3,13... | collective-permute-start | bytes 393224 | tf_op jit(solution)/shard_map/ppermute | solution.py:253
  16.9 0.0 collective-permute-done.3.refs_4_.refs_0_
  16.9 0.0 collective-permute-start.5
  16.9 0.8 %collective-permute-start.4 = (bf16[64,1024]{1,0:T(8,128)(2,1)S(1)}, bf16[64,1024]{1,0:T(8,128)(2,1)S(1)}, u32[]{:S(2)}, u32[]{:S(2)}) collective-permute-start(bf16[64,1024]{1,0:T(8,128)(2,1)S(1)} %collective-permute-done.3.refs_4_.refs_0_), channel_id=1, source_target_pairs={{0,2},{2,0},{4,6},{6,4},{8,10},{10,8},{12,14},{14,12},{1,3},{3,1},... | collective-permute-start | bytes 393224 | tf_op jit(solution)/shard_map/ppermute | solution.py:253
  17.7 0.0 collective-permute-done.8
  17.7 0.1 pad_add_fusion.cand_ref
  17.8 2.8 %collective-permute-start.9 = (s32[16,256]{1,0:T(8,128)S(1)}, s32[16,256]{1,0:T(8,128)S(1)}, u32[]{:S(2)}, u32[]{:S(2)}) collective-permute-start(s32[16,256]{1,0:T(8,128)S(1)} %pad_add_fusion.cand_ref), channel_id=1, source_target_pairs={{0,8},{2,10},{4,12},{6,14},{8,0},{10,2},{12,4},{14,6},{1,9},{3,11}... | collective-permute-start | bytes 49160 | tf_op jit(solution)/shard_map/ppermute | solution.py:253
  20.5 3.0 %collective-permute-done.9.cand_ref = s32[16,256]{1,0:T(8,128)S(1)} collective-permute-done((s32[16,256]{1,0:T(8,128)S(1)}, s32[16,256]{1,0:T(8,128)S(1)}, u32[]{:S(2)}, u32[]{:S(2)}) %collective-permute-start.9) | collective-permute-done | bytes 16416 | tf_op jit(solution)/shard_map/ppermute | solution.py:253
  23.5 0.5 %collective-permute-start = (bf16[64,1024]{1,0:T(8,128)(2,1)S(1)}, bf16[64,1024]{1,0:T(8,128)(2,1)S(1)}, u32[]{:S(2)}, u32[]{:S(2)}) collective-permute-start(bf16[64,1024]{1,0:T(8,128)(2,1)S(1)} %copy-done.2), channel_id=1, source_target_pairs={{0,2},{2,0},{4,6},{6,4},{8,10},{10,8},{12,14},{14,12},{1,3},{3,1},... | collective-permute-start | bytes 393224 | tf_op jit(solution)/shard_map/ppermute | solution.py:253
  24.0 0.0 collective-permute-done.1.refs_2_
  24.0 1.5 %collective-permute-start.2 = (bf16[64,1024]{1,0:T(8,128)(2,1)S(1)}, bf16[64,1024]{1,0:T(8,128)(2,1)S(1)}, u32[]{:S(2)}, u32[]{:S(2)}) collective-permute-start(bf16[64,1024]{1,0:T(8,128)(2,1)S(1)} %collective-permute-done.1.refs_2_), channel_id=1, source_target_pairs={{0,2},{2,0},{4,6},{6,4},{8,10},{10,8},{12,14},{14,12},{1,3},{3,1},... | collective-permute-start | bytes 393224 | tf_op jit(solution)/shard_map/ppermute | solution.py:253
  25.5 0.0 collective-permute-done.6.refs_7_.refs_3_
  25.5 0.0 collective-permute-done.5.refs_6_.refs_2_
  25.5 0.0 collective-permute-done.4.refs_5_.refs_1_
  25.5 1.5 %exact.3 = f32[16,256]{1,0:T(8,128)S(1)} custom-call(s32[16,256]{1,0:T(8,128)S(1)} %collective-permute-done.9.cand_ref, bf16[2048,1024]{1,0:T(8,128)(2,1)S(1)} %get-tuple-element.9.rows_ref, bf16[64,1024]{1,0:T(8,128)(2,1)S(1)} %collective-permute-done.3.refs_4_.refs_0_, bf16[64,1024]{1,0:T(8,128)(2,1)S(1)} %collective-permute-done.4.refs_5_.refs_1_, ...), custom_call_target="tpu_custom_call" | custom-call | flops 1073741824 | bytes 4194304 | tf_op jit(solution)/shard_map/exact/pallas_call | solution.py:172
  27.1 2.6 %collective-permute-start.10 = (f32[16,256]{1,0:T(8,128)S(1)}, f32[16,256]{1,0:T(8,128)S(1)}, u32[]{:S(2)}, u32[]{:S(2)}) collective-permute-start(f32[16,256]{1,0:T(8,128)S(1)} %exact.3), channel_id=1, source_target_pairs={{0,8},{2,10},{4,12},{6,14},{8,0},{10,2},{12,4},{14,6},{1,9},{3,11}... | collective-permute-start | bytes 49160 | tf_op jit(solution)/shard_map/ppermute | solution.py:253
  29.6 0.0 collective-permute-done.refs_1_
  29.6 0.3 collective-permute-done.2.refs_3_
  29.9 1.5 %exact.2 = f32[16,256]{1,0:T(8,128)S(1)} custom-call(s32[16,256]{1,0:T(8,128)S(1)} %pad_add_fusion.cand_ref, bf16[2048,1024]{1,0:T(8,128)(2,1)S(1)} %get-tuple-element.9.rows_ref, bf16[64,1024]{1,0:T(8,128)(2,1)S(1)} %get-tuple-element.7.refs_0_, bf16[64,1024]{1,0:T(8,128)(2,1)S(1)} %collective-permute-done.refs_1_, ...), custom_call_target="tpu_custom_call" | custom-call | flops 1073741824 | bytes 4194304 | tf_op jit(solution)/shard_map/exact/pallas_call | solution.py:172
  31.4 0.0 copy-start
  31.4 0.0 copy-start.1
  31.4 0.4 collective-permute-done.10
  31.8 2.0 %collective-permute-start.11 = (f32[16,128]{1,0:T(8,128)S(1)}, f32[16,128]{1,0:T(8,128)S(1)}, u32[]{:S(2)}, u32[]{:S(2)}) collective-permute-start(f32[16,128]{1,0:T(8,128)S(1)} %slice.20), channel_id=1, source_target_pairs={{0,4},{2,6},{4,0},{6,2},{8,12},{10,14},{12,8},{14,10},{1,5},{3,7},... | collective-permute-start | bytes 24584 | tf_op jit(solution)/shard_map/ppermute | solution.py:253
  33.8 1.7 %collective-permute-done.11 = f32[16,128]{1,0:T(8,128)S(1)} collective-permute-done((f32[16,128]{1,0:T(8,128)S(1)}, f32[16,128]{1,0:T(8,128)S(1)}, u32[]{:S(2)}, u32[]{:S(2)}) %collective-permute-start.11) | collective-permute-done | bytes 8224 | tf_op jit(solution)/shard_map/ppermute | solution.py:253
  35.4 0.1 slice.22
  35.5 1.0 %collective-permute-start.12 = (f32[16,64]{1,0:T(8,128)S(1)}, f32[16,64]{1,0:T(8,128)S(1)}, u32[]{:S(2)}, u32[]{:S(2)}) collective-permute-start(f32[16,64]{1,0:T(8,128)S(1)} %slice.22), channel_id=1, source_target_pairs={{0,2},{2,0},{4,6},{6,4},{8,10},{10,8},{12,14},{14,12},{1,3},{3,1},... | collective-permute-start | bytes 12296 | tf_op jit(solution)/shard_map/ppermute | solution.py:253
  36.5 2.6 %score_blocks.1.scores_ref = bf16[8,512,256]{2,1,0:T(8,128)(2,1)S(1)} custom-call(bf16[2048,1024]{1,0:T(8,128)(2,1)S(1)} %get-tuple-element.6.rows_ref, bf16[64,1024]{1,0:T(8,128)(2,1)S(1)} %get-tuple-element.7.refs_0_, bf16[64,1024]{1,0:T(8,128)(2,1)S(1)} %collective-permute-done.refs_1_, bf16[64,1024]{1,0:T(8,128)(2,1)S(1)} %collective-permute-done.1.refs_2_, ...), custom_call_target="tpu_custom_call" | custom-call | flops 2147483648 | bytes 4194304 | tf_op jit(solution)/shard_map/score_blocks/pallas_call | solution.py:212
  39.1 0.0 copy-done
  39.1 0.0 copy-done.1
  39.1 1.8 %choose.1 = bf16[8,4,64,256]{3,2,1,0:T(8,128)(2,1)} custom-call(s32[4,8]{1,0:T(4,128)S(1)} %bitcast.16, s32[8]{0:T(128)S(1)} %bitcast.17, bf16[8,512,256]{2,1,0:T(8,128)(2,1)S(1)} %score_blocks.1.scores_ref), custom_call_target="tpu_custom_call" | custom-call | bytes 4194304 | tf_op jit(solution)/shard_map/choose/pallas_call | solution.py:241
  40.9 0.0 collective-permute-done.12
  40.9 0.6 %slice_add_fusion = f32[16,64]{1,0:T(8,128)} fusion(f32[16,64]{1,0:T(8,128)S(1)} %collective-permute-done.12, f32[16,128]{1,0:T(8,128)S(1)} %slice_add_fusion.1), kind=kLoop, calls=%fused_computation.1 | loop fusion | flops 1024 | bytes 12288 | tf_op jit(solution)/shard_map/add | solution.py:294
  (3 shorter events, 0.0 us)
Async XLA Ops:
  0.6 13.5 %copy-start.2 = (bf16[64,1024]{1,0:T(8,128)(2,1)S(1)}, bf16[64,1024]{1,0:T(8,128)(2,1)}, u32[]{:S(2)}) copy-start(bf16[64,1024]{1,0:T(8,128)(2,1)} %queries_ref.1) | copy-start | bytes 393220
  0.6 16.3 %collective-permute-start.3 = (bf16[64,1024]{1,0:T(8,128)(2,1)}, bf16[64,1024]{1,0:T(8,128)(2,1)S(1)}, u32[]{:S(2)}, u32[]{:S(2)}) collective-permute-start(bf16[64,1024]{1,0:T(8,128)(2,1)} %queries_ref.1), channel_id=1, source_target_pairs={{0,8},{2,10},{4,12},{6,14},{8,0},{10,2},{12,4},{14,6},{1,9},{3,11}... | collective-permute-start | bytes 393224 | tf_op jit(solution)/shard_map/ppermute | solution.py:253
  8.8 3.7 %collective-permute-start.7 = (s32[16,64]{1,0:T(8,128)S(1)}, s32[16,64]{1,0:T(8,128)S(1)}, u32[]{:S(2)}, u32[]{:S(2)}) collective-permute-start(s32[16,64]{1,0:T(8,128)S(1)} %get-tuple-element.8), channel_id=1, source_target_pairs={{0,2},{2,0},{4,6},{6,4},{8,10},{10,8},{12,14},{14,12},{1,3},{3,1},... | collective-permute-start | bytes 12296 | tf_op jit(solution)/shard_map/ppermute | solution.py:253
  12.6 5.1 %collective-permute-start.8 = (s32[16,128]{1,0:T(8,128)S(1)}, s32[16,128]{1,0:T(8,128)S(1)}, u32[]{:S(2)}, u32[]{:S(2)}) collective-permute-start(s32[16,128]{1,0:T(8,128)S(1)} %pad_add_fusion.1), channel_id=1, source_target_pairs={{0,4},{2,6},{4,0},{6,2},{8,12},{10,14},{12,8},{14,10},{1,5},{3,7},... | collective-permute-start | bytes 24584 | tf_op jit(solution)/shard_map/ppermute | solution.py:253
  14.1 9.9 %collective-permute-start.1 = (bf16[64,1024]{1,0:T(8,128)(2,1)S(1)}, bf16[64,1024]{1,0:T(8,128)(2,1)S(1)}, u32[]{:S(2)}, u32[]{:S(2)}) collective-permute-start(bf16[64,1024]{1,0:T(8,128)(2,1)S(1)} %copy-done.2), channel_id=1, source_target_pairs={{0,4},{2,6},{4,0},{6,2},{8,12},{10,14},{12,8},{14,10},{1,5},{3,7},... | collective-permute-start | bytes 393224 | tf_op jit(solution)/shard_map/ppermute | solution.py:253
  14.6 10.9 %collective-permute-start.6 = (bf16[64,1024]{1,0:T(8,128)(2,1)S(1)}, bf16[64,1024]{1,0:T(8,128)(2,1)S(1)}, u32[]{:S(2)}, u32[]{:S(2)}) collective-permute-start(bf16[64,1024]{1,0:T(8,128)(2,1)S(1)} %get-tuple-element.7.refs_0_), channel_id=1, source_target_pairs={{0,14},{2,12},{4,10},{6,8},{8,6},{10,4},{12,2},{14,0},{1,15},{3,13... | collective-permute-start | bytes 393224 | tf_op jit(solution)/shard_map/ppermute | solution.py:253
  16.9 8.6 %collective-permute-start.5 = (bf16[64,1024]{1,0:T(8,128)(2,1)S(1)}, bf16[64,1024]{1,0:T(8,128)(2,1)S(1)}, u32[]{:S(2)}, u32[]{:S(2)}) collective-permute-start(bf16[64,1024]{1,0:T(8,128)(2,1)S(1)} %collective-permute-done.3.refs_4_.refs_0_), channel_id=1, source_target_pairs={{0,4},{2,6},{4,0},{6,2},{8,12},{10,14},{12,8},{14,10},{1,5},{3,7},... | collective-permute-start | bytes 393224 | tf_op jit(solution)/shard_map/ppermute | solution.py:253
  16.9 8.6 %collective-permute-start.4 = (bf16[64,1024]{1,0:T(8,128)(2,1)S(1)}, bf16[64,1024]{1,0:T(8,128)(2,1)S(1)}, u32[]{:S(2)}, u32[]{:S(2)}) collective-permute-start(bf16[64,1024]{1,0:T(8,128)(2,1)S(1)} %collective-permute-done.3.refs_4_.refs_0_), channel_id=1, source_target_pairs={{0,2},{2,0},{4,6},{6,4},{8,10},{10,8},{12,14},{14,12},{1,3},{3,1},... | collective-permute-start | bytes 393224 | tf_op jit(solution)/shard_map/ppermute | solution.py:253
  17.8 5.7 %collective-permute-start.9 = (s32[16,256]{1,0:T(8,128)S(1)}, s32[16,256]{1,0:T(8,128)S(1)}, u32[]{:S(2)}, u32[]{:S(2)}) collective-permute-start(s32[16,256]{1,0:T(8,128)S(1)} %pad_add_fusion.cand_ref), channel_id=1, source_target_pairs={{0,8},{2,10},{4,12},{6,14},{8,0},{10,2},{12,4},{14,6},{1,9},{3,11}... | collective-permute-start | bytes 49160 | tf_op jit(solution)/shard_map/ppermute | solution.py:253
  23.5 6.1 %collective-permute-start = (bf16[64,1024]{1,0:T(8,128)(2,1)S(1)}, bf16[64,1024]{1,0:T(8,128)(2,1)S(1)}, u32[]{:S(2)}, u32[]{:S(2)}) collective-permute-start(bf16[64,1024]{1,0:T(8,128)(2,1)S(1)} %copy-done.2), channel_id=1, source_target_pairs={{0,2},{2,0},{4,6},{6,4},{8,10},{10,8},{12,14},{14,12},{1,3},{3,1},... | collective-permute-start | bytes 393224 | tf_op jit(solution)/shard_map/ppermute | solution.py:253
  24.0 5.9 %collective-permute-start.2 = (bf16[64,1024]{1,0:T(8,128)(2,1)S(1)}, bf16[64,1024]{1,0:T(8,128)(2,1)S(1)}, u32[]{:S(2)}, u32[]{:S(2)}) collective-permute-start(bf16[64,1024]{1,0:T(8,128)(2,1)S(1)} %collective-permute-done.1.refs_2_), channel_id=1, source_target_pairs={{0,2},{2,0},{4,6},{6,4},{8,10},{10,8},{12,14},{14,12},{1,3},{3,1},... | collective-permute-start | bytes 393224 | tf_op jit(solution)/shard_map/ppermute | solution.py:253
  27.1 4.7 %collective-permute-start.10 = (f32[16,256]{1,0:T(8,128)S(1)}, f32[16,256]{1,0:T(8,128)S(1)}, u32[]{:S(2)}, u32[]{:S(2)}) collective-permute-start(f32[16,256]{1,0:T(8,128)S(1)} %exact.3), channel_id=1, source_target_pairs={{0,8},{2,10},{4,12},{6,14},{8,0},{10,2},{12,4},{14,6},{1,9},{3,11}... | collective-permute-start | bytes 49160 | tf_op jit(solution)/shard_map/ppermute | solution.py:253
  31.4 7.7 %copy-start = (s32[8,1,1,4]{0,3,2,1:T(4,128)S(1)}, s32[8,1,1,4]{0,3,2,1:T(4,128)}, u32[]{:S(2)}) copy-start(s32[8,1,1,4]{0,3,2,1:T(4,128)} %param.12) | copy-start | bytes 388
  31.4 7.7 %copy-start.1 = (s32[8,1,1]{0,2,1:T(1,128)S(1)}, s32[8,1,1]{0,2,1:T(1,128)}, u32[]{:S(2)}) copy-start(s32[8,1,1]{0,2,1:T(1,128)} %param.13) | copy-start | bytes 100
  31.8 3.7 %collective-permute-start.11 = (f32[16,128]{1,0:T(8,128)S(1)}, f32[16,128]{1,0:T(8,128)S(1)}, u32[]{:S(2)}, u32[]{:S(2)}) collective-permute-start(f32[16,128]{1,0:T(8,128)S(1)} %slice.20), channel_id=1, source_target_pairs={{0,4},{2,6},{4,0},{6,2},{8,12},{10,14},{12,8},{14,10},{1,5},{3,7},... | collective-permute-start | bytes 24584 | tf_op jit(solution)/shard_map/ppermute | solution.py:253
  35.5 5.4 %collective-permute-start.12 = (f32[16,64]{1,0:T(8,128)S(1)}, f32[16,64]{1,0:T(8,128)S(1)}, u32[]{:S(2)}, u32[]{:S(2)}) collective-permute-start(f32[16,64]{1,0:T(8,128)S(1)} %slice.22), channel_id=1, source_target_pairs={{0,2},{2,0},{4,6},{6,4},{8,10},{10,8},{12,14},{14,12},{1,3},{3,1},... | collective-permute-start | bytes 12296 | tf_op jit(solution)/shard_map/ppermute | solution.py:253

commit v3 on v2

v3 whole, which is shorter than its diff:
```python
import functools

import jax
import jax.numpy as jnp
from jax import lax
from jax.experimental import pallas as pl
from jax.experimental.pallas import tpu as pltpu
from jax.sharding import PartitionSpec as P

B = 256
NT = (((1,), (1,)), ((), ()))
IN_VMEM = pl.BlockSpec(memory_space=pltpu.VMEM)
IN_HBM = pl.BlockSpec(memory_space=pl.ANY)
IN_SMEM = pl.BlockSpec(memory_space=pltpu.SMEM)
EXACT_COST = 0
LIMIT = 24 * 2**20


def params():
    return pltpu.CompilerParams(vmem_limit_bytes=LIMIT)


def pick(table, index):
    return jnp.take_along_axis(table, index, axis=0, mode="promise_in_bounds")


def regroup_matrix(sub_width):
    run = 256 // sub_width
    source = lax.broadcasted_iota(jnp.int32, (256, 256), 0)
    target = lax.broadcasted_iota(jnp.int32, (256, 256), 1)
    return (source == (target % run) * sub_width + target // run).astype(jnp.bfloat16)


def pack_kernel(
    queries_ref, shard_ref, row_ref, out_ref, shard, row, sems, *, row_count
):
    query_rows, features = queries_ref.shape
    strips = features // 128
    copies = [
        pltpu.make_async_copy(shard_ref, shard, sems.at[strips]),
        pltpu.make_async_copy(row_ref, row, sems.at[strips + 1]),
    ]
    for strip in range(strips):
        copies.append(
            pltpu.make_async_copy(
                queries_ref.at[:, pl.ds(strip * 128, 128)],
                out_ref.at[pl.ds(strip * query_rows, query_rows)],
                sems.at[strip],
            )
        )
    for copy in copies:
        copy.start()
    copies[0].wait()
    copies[1].wait()
    place = shard[...] * (row_count // B) + row[...] // B
    tail = jnp.concatenate([place, row[...] % B], axis=1)
    out_ref[strips * query_rows :, :] = tail.astype(jnp.float32).astype(jnp.bfloat16)
    for copy in copies[2:]:
        copy.wait()


def pack(queries, cand_shard, cand_row, row_count):
    query_rows, features = queries.shape
    per_query = cand_row.shape[0]
    strips = features // 128
    return pl.pallas_call(
        functools.partial(pack_kernel, row_count=row_count),
        out_shape=pltpu.VMEM((strips * query_rows + per_query, 128), jnp.bfloat16),
        in_specs=[IN_HBM] * 3,
        out_specs=IN_VMEM,
        scratch_shapes=[
            pltpu.VMEM(cand_row.shape, jnp.int32),
            pltpu.VMEM(cand_row.shape, jnp.int32),
            pltpu.SemaphoreType.DMA((strips + 2,)),
        ],
        compiler_params=params(),
        cost_estimate=cost(0),
        name="pack",
    )(*map(in_hbm, (queries, cand_shard, cand_row)))


def decode_kernel(
    codes_ref, book_ref, rows_ref, out_ref, rows_out, codes, book, tables, sems, row_sems, *, step
):
    row_count, features = out_ref.shape
    code_count = codes_ref.shape[1]
    parts = row_count // step

    def fetch(part):
        here = pl.ds(pl.multiple_of(part * step, step), step)
        return pltpu.make_async_copy(codes_ref.at[here], codes.at[here], sems.at[part])

    book_copy = pltpu.make_async_copy(book_ref, book, sems.at[parts])
    book_copy.start()
    for part in range(parts):
        fetch(part).start()
    row_copies = []
    piece = row_count // row_sems.shape[0]
    for at in range(row_sems.shape[0]):
        here = pl.ds(at * piece, piece)
        row_copies.append(
            pltpu.make_async_copy(rows_ref.at[here], rows_out.at[here], row_sems.at[at])
        )
        row_copies[-1].start()
    regroup = regroup_matrix(features // code_count)
    book_copy.wait()
    for left in range(0, features, 256):
        tables[:, left : left + 256] = jnp.dot(
            book[:, left : left + 256], regroup, preferred_element_type=jnp.float32
        )

    @pl.loop(0, parts)
    def _(at):
        fetch(at).wait()
        here = pl.ds(pl.multiple_of(at * step, step), step)
        first = lax.broadcasted_iota(jnp.int32, (step, 128), 1) < 64
        for pair in range(code_count // 128):
            both = codes[here, pair * 128 : (pair + 1) * 128]
            turned = pltpu.roll(both, 64, 1)
            for side in range(2):
                index = jnp.where(first, both, turned) if side == 0 else jnp.where(first, turned, both)
                inner = index & 7
                upper = index >= 8
                for half in range(2):
                    left = (pair * 2 + side) * 256 + half * 128
                    low = tables[:8, left : left + 128]
                    high = tables[8:16, left : left + 128]
                    pieces = []
                    for top in range(0, step, 8):
                        near = slice(top, top + 8)
                        pieces.append(
                            jnp.where(upper[near], pick(high, inner[near]), pick(low, inner[near]))
                        )
                    out_ref[here, left : left + 128] = jnp.concatenate(pieces, axis=0).astype(
                        jnp.bfloat16
                    )

    for copy in row_copies:
        copy.wait()


def decode(pq_codes, codebook, full_rows):
    features = codebook.shape[1]
    rows = pq_codes.shape[0]
    step = 256
    return pl.pallas_call(
        functools.partial(decode_kernel, step=step),
        out_shape=[
            pltpu.VMEM((rows, features), jnp.bfloat16),
            pltpu.VMEM(full_rows.shape, full_rows.dtype),
        ],
        in_specs=[IN_HBM] * 3,
        out_specs=[IN_VMEM] * 2,
        scratch_shapes=[
            pltpu.VMEM(pq_codes.shape, jnp.int32),
            pltpu.VMEM(codebook.shape, codebook.dtype),
            pltpu.VMEM(codebook.shape, jnp.float32),
            pltpu.SemaphoreType.DMA((rows // step + 1,)),
            pltpu.SemaphoreType.DMA((4,)),
        ],
        compiler_params=params(),
        cost_estimate=cost(0),
        name="decode",
    )(*map(in_hbm, (pq_codes, codebook, full_rows)))


def cost(size):
    return pl.CostEstimate(flops=size * 10**9, bytes_accessed=size * 2**20, transcendentals=0)


def in_hbm(x):
    return pltpu.with_memory_space_constraint(x, pltpu.HBM)


def in_vmem(x):
    return pltpu.with_memory_space_constraint(x, pltpu.VMEM)


def count_queries(block, rows, per_query):
    return (block.shape[0] - per_query) * 128 // rows.shape[1]


def fill(stack, blocks):
    query_rows = stack.shape[0] // len(blocks)
    for at, block in enumerate(blocks):
        for strip in range(stack.shape[1] // 128):
            stack[at * query_rows : (at + 1) * query_rows, strip * 128 : (strip + 1) * 128] = block[
                strip * query_rows : (strip + 1) * query_rows, :
            ]


def find(stack, rows_ref, blocks, per_query, groups):
    row_count = rows_ref.shape[0]
    width = stack.shape[0]
    query_rows = width // len(blocks)
    tops = per_query // groups
    scores = lax.dot_general(
        rows_ref[...], stack[...], NT, preferred_element_type=jnp.float32
    )
    tails = [block[-per_query:, :].astype(jnp.int32) for block in blocks]
    wanted = jnp.concatenate(
        [tail[:, :query_rows] * B + tail[:, query_rows : 2 * query_rows] for tail in tails], axis=1
    )
    wanted = wanted - lax.axis_index("corpus") * row_count
    mine = (wanted >= 0) & (wanted < row_count)
    kept = jnp.where(mine, wanted, -1)
    down = lax.broadcasted_iota(jnp.int32, (8, width), 0)
    found = []
    for group in range(groups):
        row = jnp.max(kept[group * tops : (group + 1) * tops], axis=0, keepdims=True)
        row = jnp.broadcast_to(row, (8, width)) - down
        total = jnp.zeros((8, width), jnp.float32)
        for top in range(0, row_count, 8):
            total = jnp.where(row == top, scores[top : top + 8], total)
        total = jnp.sum(total, axis=0, keepdims=True)
        found.append(jnp.broadcast_to(total, (tops, width)))
    return jnp.where(mine, jnp.concatenate(found, axis=0), 0.0)


def score(stack, decoded_ref, out_ref, sub_width):
    regroup = regroup_matrix(sub_width)
    for left in range(0, stack.shape[1], 256):
        run = slice(left, left + 256)
        stack[:, run] = jnp.dot(
            stack[:, run], regroup, preferred_element_type=jnp.float32
        ).astype(jnp.bfloat16)
    for block in range(out_ref.shape[0]):
        out_ref[block] = lax.dot_general(
            stack[...],
            decoded_ref[block * B : (block + 1) * B, :],
            NT,
            preferred_element_type=jnp.float32,
        ).astype(jnp.bfloat16)


def exact_kernel(rows_ref, *refs, per_query, groups):
    blocks, (found_ref, stack) = refs[:-2], refs[-2:]
    fill(stack, blocks)
    found_ref[...] = find(stack, rows_ref, blocks, per_query, groups)


def exact(full_rows, blocks, groups, tops):
    per_query = groups * tops
    width = len(blocks) * count_queries(blocks[0], full_rows, per_query)
    return pl.pallas_call(
        functools.partial(exact_kernel, per_query=per_query, groups=groups),
        out_shape=pltpu.VMEM((per_query, width), jnp.float32),
        in_specs=[IN_VMEM] * (1 + len(blocks)),
        out_specs=IN_VMEM,
        scratch_shapes=[pltpu.VMEM((width, full_rows.shape[1]), jnp.bfloat16)],
        compiler_params=params(),
        cost_estimate=cost(0),
        name="exact",
    )(*map(in_vmem, [full_rows] + blocks))


def scores_kernel(decoded_ref, *refs, sub_width):
    blocks, (scores_ref, stack) = refs[:-2], refs[-2:]
    fill(stack, blocks)
    score(stack, decoded_ref, scores_ref, sub_width)


def score_blocks(decoded, blocks, sub_width, per_query):
    width = len(blocks) * count_queries(blocks[0], decoded, per_query)
    rows, features = decoded.shape
    return pl.pallas_call(
        functools.partial(scores_kernel, sub_width=sub_width),
        out_shape=pltpu.VMEM((rows // B, width, B), jnp.bfloat16),
        in_specs=[IN_VMEM] * (1 + len(blocks)),
        out_specs=IN_VMEM,
        scratch_shapes=[pltpu.VMEM((width, features), jnp.bfloat16)],
        compiler_params=params(),
        cost_estimate=cost(0),
        name="score_blocks",
    )(*map(in_vmem, [decoded] + blocks))


def place_scores(ids_ref, len_ref, scores_ref, out_ref, owners):
    query_rows = out_ref.shape[2]
    for at, owner in enumerate(owners):
        here = slice(at * query_rows, (at + 1) * query_rows)
        for slot in range(out_ref.shape[1]):
            picked = scores_ref[ids_ref[slot, owner], here, :]
            out_ref[owner, slot] = jnp.where(slot < len_ref[owner], picked, jnp.zeros_like(picked))


def late_approx_kernel(
    ids_ref, len_ref, decoded_ref, scores_ref, *refs, places, sub_width
):
    blocks, (out_ref, stack, late_scores) = refs[:-3], refs[-3:]
    fill(stack, blocks)
    me = lax.axis_index("corpus")
    owners = [me ^ place for place in places]
    half = len(places) // 2
    place_scores(ids_ref, len_ref, scores_ref, out_ref, owners[:half])
    score(stack, decoded_ref, late_scores, sub_width)
    place_scores(ids_ref, len_ref, late_scores, out_ref, owners[half:])


def late_approx(probe_ids, probe_len, decoded, scores, blocks, places, sub_width):
    block_count, width, _ = scores.shape
    slots = probe_ids.shape[0]
    query_rows = width // len(blocks)
    return pl.pallas_call(
        functools.partial(late_approx_kernel, places=places, sub_width=sub_width),
        out_shape=pltpu.VMEM((len(places), slots, query_rows, B), jnp.bfloat16),
        in_specs=[IN_SMEM] * 2 + [IN_VMEM] * (2 + len(blocks)),
        out_specs=IN_VMEM,
        scratch_shapes=[
            pltpu.VMEM((width, decoded.shape[1]), jnp.bfloat16),
            pltpu.VMEM(scores.shape, jnp.bfloat16),
        ],
        compiler_params=params(),
        cost_estimate=cost(10),
        name="late_approx",
    )(probe_ids, probe_len, *map(in_vmem, [decoded, scores] + blocks))


def choose_kernel(ids_ref, len_ref, scores_ref, out_ref):
    place_scores(ids_ref, len_ref, scores_ref, out_ref, range(out_ref.shape[0]))


def choose(probe_ids, probe_len, scores):
    slots, count = probe_ids.shape
    query_rows = scores.shape[1] // count
    return pl.pallas_call(
        choose_kernel,
        out_shape=jax.ShapeDtypeStruct((count, slots, query_rows, B), jnp.bfloat16),
        in_specs=[IN_SMEM] * 2 + [IN_VMEM],
        out_specs=IN_VMEM,
        compiler_params=params(),
        name="choose",
    )(probe_ids, probe_len, scores)


def swap(x, distance, shards):
    return lax.ppermute(x, "corpus", [(i, i ^ distance) for i in range(shards)])


def local(queries, codebook, pq_codes, full_rows, probe_ids, probe_len, cand_shard, cand_row):
    shards = lax.axis_size("corpus")
    query_rows, features = queries.shape
    row_count = full_rows.shape[0]
    groups, tops = cand_shard.shape[1:]
    per_query = groups * tops
    slots = probe_ids.shape[-1]
    sub_width = features // pq_codes.shape[1]
    ids = probe_ids.reshape(shards, slots).T
    lens = probe_len.reshape(shards)
    own = pack(
        queries,
        cand_shard.reshape(query_rows, per_query).T,
        cand_row.reshape(query_rows, per_query).T,
        row_count,
    )

    if shards == 8:
        hold = lax.optimization_barrier
        far = swap(own, 4, shards)
        side = swap(own, 1, shards)
        near = swap(own, 2, shards)
        near_side = swap(own, 3, shards)
        decoded, rows = decode(pq_codes, codebook, full_rows)
        own_late, decoded = hold((own, decoded))
        far, decoded = hold((far, decoded))
        cross = swap(own_late, 7, shards)
        far_side = swap(far, 1, shards)
        far_near = swap(far, 2, shards)
        blocks = [own, side, near, near_side]
        found = exact(rows, blocks, groups, tops)
        scores = score_blocks(decoded, blocks, sub_width, per_query)
        far_side, far_near, cross, found, scores = hold(
            (far_side, far_near, cross, found, scores)
        )
        blocks = [far, far_side, far_near, cross]
        sent = exact(rows, blocks, groups, tops)
        approx_scores = late_approx(
            ids, lens, decoded, scores, blocks, list(range(8)), sub_width
        )
        kept = found + swap(sent, 4, shards)
        kept, approx_scores = hold((kept, approx_scores))
        parts = [kept[:, p * query_rows : (p + 1) * query_rows] for p in range(4)]
        total = parts[0]
        for distance in (1, 2, 3):
            total = total + swap(parts[distance], distance, shards)
    else:
        gathered = lax.all_gather(own, "corpus", axis=0)
        decoded, rows = decode(pq_codes, codebook, full_rows)
        answers, pieces = [], []
        step = 4
        for first in range(0, shards, step):
            blocks = [gathered[p] for p in range(first, first + step)]
            found = exact(rows, blocks, groups, tops)
            scores = score_blocks(decoded, blocks, sub_width, per_query)
            answers += [found[:, p * query_rows : (p + 1) * query_rows] for p in range(step)]
            some = slice(first, first + step)
            pieces.append(choose(ids[:, some], lens[some], scores))
        approx_scores = jnp.concatenate(pieces, axis=0)
        back = lax.all_to_all(jnp.stack(answers), "corpus", 0, 0, tiled=True)
        total = jnp.sum(back, axis=0)

    approx_scores = approx_scores.reshape(shards, 1, 1, slots, query_rows, B)
    return approx_scores, total.T.reshape(query_rows, groups, tops)


def solution(mesh):
    return jax.shard_map(
        local,
        mesh=mesh,
        in_specs=(
            P(("groups", "corpus", "replica"), None),
            P("groups", None),
            P(("groups", "corpus"), None),
            P(("groups", "corpus"), None),
            P("groups", "replica", "corpus", None),
            P("groups", "replica", "corpus"),
            P(("groups", "corpus", "replica"), None, None),
            P(("groups", "corpus", "replica"), None, None),
        ),
        out_specs=(
            P("groups", "replica", "corpus", None, None, None),
            P(("groups", "corpus", "replica"), None, None),
        ),
        check_vma=False,
    )
```

time: 41.6 us -> 35.3 us (0.85)
  starting transfers between devices: 21.1 us -> 15.6 us
  waiting for transfers between devices: 7.39 us -> 5.89 us
  local copies, waits for them, and re-layouts: 0.1 us -> 1.06 us
    ppermute x13 -> x11, starting transfers between devices: 21.1 us -> 15.6 us  [swap(): return lax.ppermute(x, 'corpus', [(i, i ^ distance) for i in range(shards)])]
    ppermute x13 -> x11, waiting for transfers between devices: 7.39 us -> 5.89 us  [swap(): return lax.ppermute(x, 'corpus', [(i, i ^ distance) for i in range(shards)])]
    pallas_call x3 -> x4, Pallas kernels: 4.78 us -> 6.07 us  [the longest x2 3.04 us: exact(): pl.pallas_call(functools.partial(exact_kernel, per_query=per_query, group...]
    pallas_call x1, Pallas kernels: 2.61 us -> 1.41 us  [score_blocks(): pl.pallas_call(functools.partial(scores_kernel, sub_width=sub_width), out...]
    unnamed x6 -> x5, local copies, waits for them, and re-layouts: 0.02 us -> 0.98 us
  transfers between devices with their start and end apart: 13 -> 11, of which waited for: 5 -> 7; matrix products, arithmetic and copies ran while one was open for 0% -> 3% of each run, Pallas kernels for 27% -> 25%
where the time goes in v3:
time: 35.3 us; the launch traced here: 35.1 us
  starting transfers between devices  15.6 us (44%)
  Pallas kernels  11.2 us (32%)
  waiting for transfers between devices  5.89 us (17%)
  local copies, waits for them, and re-layouts  1.06 us (3%)
  between operations  0.71 us (2%)
  other arithmetic  0.61 us (2%)
    ppermute x11, starting transfers between devices, swap(): return lax.ppermute(x, 'corpus', [(i, i ^ distance) for i in range(shards)])  15.6 us
    ppermute x11, waiting for transfers between devices, swap(): return lax.ppermute(x, 'corpus', [(i, i ^ distance) for i in range(shards)])  5.89 us
    pallas_call x1, Pallas kernels, decode(): pl.pallas_call(functools.partial(decode_kernel, step=step), out_shape=[pl...  3.69 us
    pallas_call x2, Pallas kernels, exact(): pl.pallas_call(functools.partial(exact_kernel, per_query=per_query, group...  3.04 us
    pallas_call x1, Pallas kernels, late_approx(): pl.pallas_call(functools.partial(late_approx_kernel, places=places, sub_w...  2.07 us
    pallas_call x1, Pallas kernels, score_blocks(): pl.pallas_call(functools.partial(scores_kernel, sub_width=sub_width), out...  1.41 us
    unnamed x5, local copies, waits for them, and re-layouts  0.98 us
    pallas_call x1, Pallas kernels, pack(): pl.pallas_call(functools.partial(pack_kernel, row_count=row_count), out_s...  0.95 us
  transfers between devices with their start and end apart: 11, of which 7 were waited for; matrix products, arithmetic and copies ran while one was open for 3% of the time, Pallas kernels for 25%

profile of v3, /device:TPU:0, one launch (start us, length us, event | category | flops | bytes accessed | tf_op | source)
XLA Modules:
  0.0 35.1 jit_solution(12546970175132908537)
XLA Ops:
  0.6 0.9 %pack.1.refs_0_ = bf16[528,128]{1,0:T(8,128)(2,1)S(1)} custom-call(bf16[64,1024]{1,0:T(8,128)(2,1)} %queries_ref.1, s32[16,64]{1,0:T(8,128)} %bitcast.19, s32[16,64]{1,0:T(8,128)} %bitcast.20), custom_call_target="tpu_custom_call" | custom-call | tf_op jit(solution)/shard_map/pack/pallas_call | solution.py:66
  1.6 4.1 %collective-permute-start = (bf16[528,128]{1,0:T(8,128)(2,1)S(1)}, bf16[528,128]{1,0:T(8,128)(2,1)S(1)}, u32[]{:S(2)}, u32[]{:S(2)}) collective-permute-start(bf16[528,128]{1,0:T(8,128)(2,1)S(1)} %pack.1.refs_0_), channel_id=1, source_target_pairs={{0,8},{2,10},{4,12},{6,14},{8,0},{10,2},{12,4},{14,6},{1,9},{3,11}... | collective-permute-start | bytes 405512 | tf_op jit(solution)/shard_map/ppermute | solution.py:337
  5.7 2.5 %collective-permute-start.6 = (bf16[528,128]{1,0:T(8,128)(2,1)S(1)}, bf16[528,128]{1,0:T(8,128)(2,1)S(1)}, u32[]{:S(2)}, u32[]{:S(2)}) collective-permute-start(bf16[528,128]{1,0:T(8,128)(2,1)S(1)} %pack.1.refs_0_), channel_id=1, source_target_pairs={{0,6},{2,4},{4,2},{6,0},{8,14},{10,12},{12,10},{14,8},{1,7},{3,5},... | collective-permute-start | bytes 405512 | tf_op jit(solution)/shard_map/ppermute | solution.py:337
  8.2 0.4 %collective-permute-start.5 = (bf16[528,128]{1,0:T(8,128)(2,1)S(1)}, bf16[528,128]{1,0:T(8,128)(2,1)S(1)}, u32[]{:S(2)}, u32[]{:S(2)}) collective-permute-start(bf16[528,128]{1,0:T(8,128)(2,1)S(1)} %pack.1.refs_0_), channel_id=1, source_target_pairs={{0,4},{2,6},{4,0},{6,2},{8,12},{10,14},{12,8},{14,10},{1,5},{3,7},... | collective-permute-start | bytes 405512 | tf_op jit(solution)/shard_map/ppermute | solution.py:337
  8.7 0.5 %collective-permute-start.4 = (bf16[528,128]{1,0:T(8,128)(2,1)S(1)}, bf16[528,128]{1,0:T(8,128)(2,1)S(1)}, u32[]{:S(2)}, u32[]{:S(2)}) collective-permute-start(bf16[528,128]{1,0:T(8,128)(2,1)S(1)} %pack.1.refs_0_), channel_id=1, source_target_pairs={{0,2},{2,0},{4,6},{6,4},{8,10},{10,8},{12,14},{14,12},{1,3},{3,1},... | collective-permute-start | bytes 405512 | tf_op jit(solution)/shard_map/ppermute | solution.py:337
  9.2 3.7 %decode.1 = (bf16[2048,1024]{1,0:T(8,128)(2,1)S(1)}, bf16[2048,1024]{1,0:T(8,128)(2,1)S(1)}) custom-call(s32[2048,256]{1,0:T(8,128)} %codes_ref.1, bf16[16,1024]{1,0:T(8,128)(2,1)} %book_ref.1, bf16[2048,1024]{1,0:T(8,128)(2,1)} %rows_ref.1), custom_call_target="tpu_custom_call" | custom-call | tf_op jit(solution)/shard_map/decode/pallas_call | solution.py:146
  12.9 2.4 %collective-permute-start.3 = (bf16[528,128]{1,0:T(8,128)(2,1)S(1)}, bf16[528,128]{1,0:T(8,128)(2,1)S(1)}, u32[]{:S(2)}, u32[]{:S(2)}) collective-permute-start(bf16[528,128]{1,0:T(8,128)(2,1)S(1)} %pack.1.refs_0_), channel_id=1, source_target_pairs={{0,14},{2,12},{4,10},{6,8},{8,6},{10,4},{12,2},{14,0},{1,15},{3,13... | collective-permute-start | bytes 405512 | tf_op jit(solution)/shard_map/ppermute | solution.py:337
  15.2 0.0 collective-permute-done.refs_0_
  15.2 0.0 collective-permute-start.2
  15.3 0.0 collective-permute-done.6.refs_3_
  15.3 0.9 %collective-permute-start.1 = (bf16[528,128]{1,0:T(8,128)(2,1)S(1)}, bf16[528,128]{1,0:T(8,128)(2,1)S(1)}, u32[]{:S(2)}, u32[]{:S(2)}) collective-permute-start(bf16[528,128]{1,0:T(8,128)(2,1)S(1)} %collective-permute-done.refs_0_), channel_id=1, source_target_pairs={{0,2},{2,0},{4,6},{6,4},{8,10},{10,8},{12,14},{14,12},{1,3},{3,1},... | collective-permute-start | bytes 405512 | tf_op jit(solution)/shard_map/ppermute | solution.py:337
  16.1 0.2 collective-permute-done.5.refs_2_
  16.3 0.0 collective-permute-done.4.refs_1_
  16.3 1.5 %exact.2 = f32[16,256]{1,0:T(8,128)S(1)} custom-call(bf16[2048,1024]{1,0:T(8,128)(2,1)S(1)} %get-tuple-element.19.rows_ref, bf16[528,128]{1,0:T(8,128)(2,1)S(1)} %pack.1.refs_0_, bf16[528,128]{1,0:T(8,128)(2,1)S(1)} %collective-permute-done.4.refs_1_, bf16[528,128]{1,0:T(8,128)(2,1)S(1)} %collective-permute-done.5.refs_2_, ...), custom_call_target="tpu_custom_call" | custom-call | tf_op jit(solution)/shard_map/exact/pallas_call | solution.py:245
  17.9 0.0 copy-start
  17.9 0.0 copy-start.1
  17.9 1.4 %score_blocks.1.scores_ref = bf16[8,256,256]{2,1,0:T(8,128)(2,1)S(1)} custom-call(bf16[2048,1024]{1,0:T(8,128)(2,1)S(1)} %get-tuple-element.20.decoded_ref, bf16[528,128]{1,0:T(8,128)(2,1)S(1)} %pack.1.refs_0_, bf16[528,128]{1,0:T(8,128)(2,1)S(1)} %collective-permute-done.4.refs_1_, bf16[528,128]{1,0:T(8,128)(2,1)S(1)} %collective-permute-done.5.refs_2_, ...), custom_call_target="tpu_custom_call" | custom-call | tf_op jit(solution)/shard_map/score_blocks/pallas_call | solution.py:266
  19.3 2.4 %collective-permute-done.3.refs_3_ = bf16[528,128]{1,0:T(8,128)(2,1)S(1)} collective-permute-done((bf16[528,128]{1,0:T(8,128)(2,1)S(1)}, bf16[528,128]{1,0:T(8,128)(2,1)S(1)}, u32[]{:S(2)}, u32[]{:S(2)}) %collective-permute-start.3) | collective-permute-done | bytes 135200 | tf_op jit(solution)/shard_map/ppermute | solution.py:337
  21.7 0.4 %collective-permute-done.2.refs_2_ = bf16[528,128]{1,0:T(8,128)(2,1)S(1)} collective-permute-done((bf16[528,128]{1,0:T(8,128)(2,1)S(1)}, bf16[528,128]{1,0:T(8,128)(2,1)S(1)}, u32[]{:S(2)}, u32[]{:S(2)}) %collective-permute-start.2) | collective-permute-done | bytes 135200 | tf_op jit(solution)/shard_map/ppermute | solution.py:337
  22.1 0.1 collective-permute-done.1.refs_1_
  22.2 1.5 %exact.3 = f32[16,256]{1,0:T(8,128)S(1)} custom-call(bf16[2048,1024]{1,0:T(8,128)(2,1)S(1)} %get-tuple-element.19.rows_ref, bf16[528,128]{1,0:T(8,128)(2,1)S(1)} %collective-permute-done.refs_0_, bf16[528,128]{1,0:T(8,128)(2,1)S(1)} %collective-permute-done.1.refs_1_, bf16[528,128]{1,0:T(8,128)(2,1)S(1)} %collective-permute-done.2.refs_2_, ...), custom_call_target="tpu_custom_call" | custom-call | tf_op jit(solution)/shard_map/exact/pallas_call | solution.py:245
  23.7 1.3 %collective-permute-start.7 = (f32[16,256]{1,0:T(8,128)S(1)}, f32[16,256]{1,0:T(8,128)S(1)}, u32[]{:S(2)}, u32[]{:S(2)}) collective-permute-start(f32[16,256]{1,0:T(8,128)S(1)} %exact.3), channel_id=1, source_target_pairs={{0,8},{2,10},{4,12},{6,14},{8,0},{10,2},{12,4},{14,6},{1,9},{3,11}... | collective-permute-start | bytes 49160 | tf_op jit(solution)/shard_map/ppermute | solution.py:337
  25.0 0.0 copy-done
  25.0 0.0 copy-done.1
  25.0 2.1 %late_approx.1 = bf16[8,4,64,256]{3,2,1,0:T(8,128)(2,1)S(1)} custom-call(s32[4,8]{1,0:T(4,128)S(1)} %bitcast.17, s32[8]{0:T(128)S(1)} %bitcast.18, bf16[2048,1024]{1,0:T(8,128)(2,1)S(1)} %get-tuple-element.20.decoded_ref, bf16[8,256,256]{2,1,0:T(8,128)(2,1)S(1)} %score_blocks.1.scores_ref, bf16[528,128]{1,0:T(8,128)(2,1)S(1)} %collective-permute-done.refs_0_, ...), custom_call_target="tpu_custom_call" | custom-call | flops 10000000000 | bytes 10485760 | tf_op jit(solution)/shard_map/late_approx/pallas_call | solution.py:304
  27.1 1.3 %collective-permute-done.7 = f32[16,256]{1,0:T(8,128)S(1)} collective-permute-done((f32[16,256]{1,0:T(8,128)S(1)}, f32[16,256]{1,0:T(8,128)S(1)}, u32[]{:S(2)}, u32[]{:S(2)}) %collective-permute-start.7) | collective-permute-done | bytes 16416 | tf_op jit(solution)/shard_map/ppermute | solution.py:337
  28.4 0.1 fusion
  28.5 0.9 %collective-permute-start.8 = (f32[16,64]{1,0:T(8,128)S(1)}, f32[16,64]{1,0:T(8,128)S(1)}, u32[]{:S(2)}, u32[]{:S(2)}) collective-permute-start(f32[16,64]{1,0:T(8,128)S(1)} %get-tuple-element.30), channel_id=1, source_target_pairs={{0,2},{2,0},{4,6},{6,4},{8,10},{10,8},{12,14},{14,12},{1,3},{3,1},... | collective-permute-start | bytes 12296 | tf_op jit(solution)/shard_map/ppermute | solution.py:337
  29.3 1.5 %collective-permute-start.10 = (f32[16,64]{1,0:T(8,128)S(1)}, f32[16,64]{1,0:T(8,128)S(1)}, u32[]{:S(2)}, u32[]{:S(2)}) collective-permute-start(f32[16,64]{1,0:T(8,128)S(1)} %get-tuple-element.31), channel_id=1, source_target_pairs={{0,6},{2,4},{4,2},{6,0},{8,14},{10,12},{12,10},{14,8},{1,7},{3,5},... | collective-permute-start | bytes 12296 | tf_op jit(solution)/shard_map/ppermute | solution.py:337
  30.8 1.2 %collective-permute-start.9 = (f32[16,64]{1,0:T(8,128)S(1)}, f32[16,64]{1,0:T(8,128)S(1)}, u32[]{:S(2)}, u32[]{:S(2)}) collective-permute-start(f32[16,64]{1,0:T(8,128)S(1)} %get-tuple-element.32), channel_id=1, source_target_pairs={{0,4},{2,6},{4,0},{6,2},{8,12},{10,14},{12,8},{14,10},{1,5},{3,7},... | collective-permute-start | bytes 12296 | tf_op jit(solution)/shard_map/ppermute | solution.py:337
  32.0 1.0 %copy.11 = bf16[8,1,1,4,64,256]{5,4,3,2,1,0:T(8,128)(2,1)} copy(bf16[8,1,1,4,64,256]{5,4,3,2,1,0:T(8,128)(2,1)S(1)} %bitcast.16) | data formatting | bytes 2097152
  32.9 0.0 collective-permute-done.8
  32.9 0.9 %collective-permute-done.10 = f32[16,64]{1,0:T(8,128)S(1)} collective-permute-done((f32[16,64]{1,0:T(8,128)S(1)}, f32[16,64]{1,0:T(8,128)S(1)}, u32[]{:S(2)}, u32[]{:S(2)}) %collective-permute-start.10) | collective-permute-done | bytes 4128 | tf_op jit(solution)/shard_map/ppermute | solution.py:337
  33.9 0.6 %collective-permute-done.9 = f32[16,64]{1,0:T(8,128)S(1)} collective-permute-done((f32[16,64]{1,0:T(8,128)S(1)}, f32[16,64]{1,0:T(8,128)S(1)}, u32[]{:S(2)}, u32[]{:S(2)}) %collective-permute-start.9) | collective-permute-done | bytes 4128 | tf_op jit(solution)/shard_map/ppermute | solution.py:337
  34.5 0.6 %add_add_fusion = f32[16,64]{1,0:T(8,128)} fusion(f32[16,64]{1,0:T(8,128)S(1)} %collective-permute-done.10, f32[16,64]{1,0:T(8,128)S(1)} %collective-permute-done.9, f32[16,64]{1,0:T(8,128)S(1)} %collective-permute-done.8, f32[16,256]{1,0:T(8,128)S(1)} %add.12), kind=kLoop, calls=%fused_computation | loop fusion | flops 3072 | bytes 20480 | tf_op jit(solution)/shard_map/add | solution.py:385
  (1 shorter events, 0.0 us)
Async XLA Ops:
  1.6 13.7 %collective-permute-start = (bf16[528,128]{1,0:T(8,128)(2,1)S(1)}, bf16[528,128]{1,0:T(8,128)(2,1)S(1)}, u32[]{:S(2)}, u32[]{:S(2)}) collective-permute-start(bf16[528,128]{1,0:T(8,128)(2,1)S(1)} %pack.1.refs_0_), channel_id=1, source_target_pairs={{0,8},{2,10},{4,12},{6,14},{8,0},{10,2},{12,4},{14,6},{1,9},{3,11}... | collective-permute-start | bytes 405512 | tf_op jit(solution)/shard_map/ppermute | solution.py:337
  5.7 9.6 %collective-permute-start.6 = (bf16[528,128]{1,0:T(8,128)(2,1)S(1)}, bf16[528,128]{1,0:T(8,128)(2,1)S(1)}, u32[]{:S(2)}, u32[]{:S(2)}) collective-permute-start(bf16[528,128]{1,0:T(8,128)(2,1)S(1)} %pack.1.refs_0_), channel_id=1, source_target_pairs={{0,6},{2,4},{4,2},{6,0},{8,14},{10,12},{12,10},{14,8},{1,7},{3,5},... | collective-permute-start | bytes 405512 | tf_op jit(solution)/shard_map/ppermute | solution.py:337
  8.2 8.1 %collective-permute-start.5 = (bf16[528,128]{1,0:T(8,128)(2,1)S(1)}, bf16[528,128]{1,0:T(8,128)(2,1)S(1)}, u32[]{:S(2)}, u32[]{:S(2)}) collective-permute-start(bf16[528,128]{1,0:T(8,128)(2,1)S(1)} %pack.1.refs_0_), channel_id=1, source_target_pairs={{0,4},{2,6},{4,0},{6,2},{8,12},{10,14},{12,8},{14,10},{1,5},{3,7},... | collective-permute-start | bytes 405512 | tf_op jit(solution)/shard_map/ppermute | solution.py:337
  8.7 7.7 %collective-permute-start.4 = (bf16[528,128]{1,0:T(8,128)(2,1)S(1)}, bf16[528,128]{1,0:T(8,128)(2,1)S(1)}, u32[]{:S(2)}, u32[]{:S(2)}) collective-permute-start(bf16[528,128]{1,0:T(8,128)(2,1)S(1)} %pack.1.refs_0_), channel_id=1, source_target_pairs={{0,2},{2,0},{4,6},{6,4},{8,10},{10,8},{12,14},{14,12},{1,3},{3,1},... | collective-permute-start | bytes 405512 | tf_op jit(solution)/shard_map/ppermute | solution.py:337
  12.9 8.8 %collective-permute-start.3 = (bf16[528,128]{1,0:T(8,128)(2,1)S(1)}, bf16[528,128]{1,0:T(8,128)(2,1)S(1)}, u32[]{:S(2)}, u32[]{:S(2)}) collective-permute-start(bf16[528,128]{1,0:T(8,128)(2,1)S(1)} %pack.1.refs_0_), channel_id=1, source_target_pairs={{0,14},{2,12},{4,10},{6,8},{8,6},{10,4},{12,2},{14,0},{1,15},{3,13... | collective-permute-start | bytes 405512 | tf_op jit(solution)/shard_map/ppermute | solution.py:337
  15.2 6.9 %collective-permute-start.2 = (bf16[528,128]{1,0:T(8,128)(2,1)S(1)}, bf16[528,128]{1,0:T(8,128)(2,1)S(1)}, u32[]{:S(2)}, u32[]{:S(2)}) collective-permute-start(bf16[528,128]{1,0:T(8,128)(2,1)S(1)} %collective-permute-done.refs_0_), channel_id=1, source_target_pairs={{0,4},{2,6},{4,0},{6,2},{8,12},{10,14},{12,8},{14,10},{1,5},{3,7},... | collective-permute-start | bytes 405512 | tf_op jit(solution)/shard_map/ppermute | solution.py:337
  15.3 6.9 %collective-permute-start.1 = (bf16[528,128]{1,0:T(8,128)(2,1)S(1)}, bf16[528,128]{1,0:T(8,128)(2,1)S(1)}, u32[]{:S(2)}, u32[]{:S(2)}) collective-permute-start(bf16[528,128]{1,0:T(8,128)(2,1)S(1)} %collective-permute-done.refs_0_), channel_id=1, source_target_pairs={{0,2},{2,0},{4,6},{6,4},{8,10},{10,8},{12,14},{14,12},{1,3},{3,1},... | collective-permute-start | bytes 405512 | tf_op jit(solution)/shard_map/ppermute | solution.py:337
  17.9 7.2 %copy-start = (s32[8,1,1,4]{0,3,2,1:T(4,128)S(1)}, s32[8,1,1,4]{0,3,2,1:T(4,128)}, u32[]{:S(2)}) copy-start(s32[8,1,1,4]{0,3,2,1:T(4,128)} %param.12) | copy-start | bytes 388
  17.9 7.1 %copy-start.1 = (s32[8,1,1]{0,2,1:T(1,128)S(1)}, s32[8,1,1]{0,2,1:T(1,128)}, u32[]{:S(2)}) copy-start(s32[8,1,1]{0,2,1:T(1,128)} %param.13) | copy-start | bytes 100
  23.7 4.7 %collective-permute-start.7 = (f32[16,256]{1,0:T(8,128)S(1)}, f32[16,256]{1,0:T(8,128)S(1)}, u32[]{:S(2)}, u32[]{:S(2)}) collective-permute-start(f32[16,256]{1,0:T(8,128)S(1)} %exact.3), channel_id=1, source_target_pairs={{0,8},{2,10},{4,12},{6,14},{8,0},{10,2},{12,4},{14,6},{1,9},{3,11}... | collective-permute-start | bytes 49160 | tf_op jit(solution)/shard_map/ppermute | solution.py:337
  28.5 4.5 %collective-permute-start.8 = (f32[16,64]{1,0:T(8,128)S(1)}, f32[16,64]{1,0:T(8,128)S(1)}, u32[]{:S(2)}, u32[]{:S(2)}) collective-permute-start(f32[16,64]{1,0:T(8,128)S(1)} %get-tuple-element.30), channel_id=1, source_target_pairs={{0,2},{2,0},{4,6},{6,4},{8,10},{10,8},{12,14},{14,12},{1,3},{3,1},... | collective-permute-start | bytes 12296 | tf_op jit(solution)/shard_map/ppermute | solution.py:337
  29.3 4.5 %collective-permute-start.10 = (f32[16,64]{1,0:T(8,128)S(1)}, f32[16,64]{1,0:T(8,128)S(1)}, u32[]{:S(2)}, u32[]{:S(2)}) collective-permute-start(f32[16,64]{1,0:T(8,128)S(1)} %get-tuple-element.31), channel_id=1, source_target_pairs={{0,6},{2,4},{4,2},{6,0},{8,14},{10,12},{12,10},{14,8},{1,7},{3,5},... | collective-permute-start | bytes 12296 | tf_op jit(solution)/shard_map/ppermute | solution.py:337
  30.8 3.7 %collective-permute-start.9 = (f32[16,64]{1,0:T(8,128)S(1)}, f32[16,64]{1,0:T(8,128)S(1)}, u32[]{:S(2)}, u32[]{:S(2)}) collective-permute-start(f32[16,64]{1,0:T(8,128)S(1)} %get-tuple-element.32), channel_id=1, source_target_pairs={{0,4},{2,6},{4,0},{6,2},{8,12},{10,14},{12,8},{14,10},{1,5},{3,7},... | collective-permute-start | bytes 12296 | tf_op jit(solution)/shard_map/ppermute | solution.py:337

commit v4 on v3

--- a/solution.py
+++ b/solution.py
@@ -21,7 +21,20 @@
 
 
 def pick(table, index):
-    return jnp.take_along_axis(table, index, axis=0, mode="promise_in_bounds")
+    dims = lax.GatherDimensionNumbers(
+        offset_dims=(),
+        collapsed_slice_dims=(0,),
+        start_index_map=(0,),
+        operand_batching_dims=(1,),
+        start_indices_batching_dims=(1,),
+    )
+    return lax.gather(
+        table,
+        index[..., None],
+        dims,
+        slice_sizes=(1, 1),
+        mode=lax.GatherScatterMode.PROMISE_IN_BOUNDS,
+    )
 
 
 def regroup_matrix(sub_width):
@@ -83,7 +96,7 @@
     codes_ref, book_ref, rows_ref, out_ref, rows_out, codes, book, tables, sems, row_sems, *, step
 ):
     row_count, features = out_ref.shape
-    code_count = codes_ref.shape[1]
+    centroids, code_count = book_ref.shape[0], codes_ref.shape[1]
     parts = row_count // step
 
     def fetch(part):
@@ -107,7 +120,7 @@
     for left in range(0, features, 256):
         tables[:, left : left + 256] = jnp.dot(
             book[:, left : left + 256], regroup, preferred_element_type=jnp.float32
-        )
+        ).astype(jnp.bfloat16)
 
     @pl.loop(0, parts)
     def _(at):
@@ -119,21 +132,15 @@
             turned = pltpu.roll(both, 64, 1)
             for side in range(2):
                 index = jnp.where(first, both, turned) if side == 0 else jnp.where(first, turned, both)
-                inner = index & 7
-                upper = index >= 8
+                index = index.astype(jnp.int16)
                 for half in range(2):
                     left = (pair * 2 + side) * 256 + half * 128
-                    low = tables[:8, left : left + 128]
-                    high = tables[8:16, left : left + 128]
-                    pieces = []
-                    for top in range(0, step, 8):
-                        near = slice(top, top + 8)
-                        pieces.append(
-                            jnp.where(upper[near], pick(high, inner[near]), pick(low, inner[near]))
-                        )
-                    out_ref[here, left : left + 128] = jnp.concatenate(pieces, axis=0).astype(
-                        jnp.bfloat16
-                    )
+                    table = tables[:, left : left + 128]
+                    pieces = [
+                        pick(table, index[top : top + centroids])
+                        for top in range(0, step, centroids)
+                    ]
+                    out_ref[here, left : left + 128] = jnp.concatenate(pieces, axis=0)
 
     for copy in row_copies:
         copy.wait()
@@ -142,7 +149,7 @@
 def decode(pq_codes, codebook, full_rows):
     features = codebook.shape[1]
     rows = pq_codes.shape[0]
-    step = 256
+    step = 512
     return pl.pallas_call(
         functools.partial(decode_kernel, step=step),
         out_shape=[
@@ -154,7 +161,7 @@
         scratch_shapes=[
             pltpu.VMEM(pq_codes.shape, jnp.int32),
             pltpu.VMEM(codebook.shape, codebook.dtype),
-            pltpu.VMEM(codebook.shape, jnp.float32),
+            pltpu.VMEM(codebook.shape, codebook.dtype),
             pltpu.SemaphoreType.DMA((rows // step + 1,)),
             pltpu.SemaphoreType.DMA((4,)),
         ],
@@ -366,23 +373,23 @@
         cross = swap(own_late, 7, shards)
         far_side = swap(far, 1, shards)
         far_near = swap(far, 2, shards)
-        blocks = [own, side, near, near_side]
+        blocks = [own, near, side, near_side]
         found = exact(rows, blocks, groups, tops)
         scores = score_blocks(decoded, blocks, sub_width, per_query)
         far_side, far_near, cross, found, scores = hold(
             (far_side, far_near, cross, found, scores)
         )
-        blocks = [far, far_side, far_near, cross]
+        blocks = [far, far_near, far_side, cross]
         sent = exact(rows, blocks, groups, tops)
         approx_scores = late_approx(
-            ids, lens, decoded, scores, blocks, list(range(8)), sub_width
+            ids, lens, decoded, scores, blocks, [0, 2, 1, 3, 4, 6, 5, 7], sub_width
         )
         kept = found + swap(sent, 4, shards)
         kept, approx_scores = hold((kept, approx_scores))
         parts = [kept[:, p * query_rows : (p + 1) * query_rows] for p in range(4)]
         total = parts[0]
-        for distance in (1, 2, 3):
-            total = total + swap(parts[distance], distance, shards)
+        for at, distance in [(3, 3), (2, 1), (1, 2)]:
+            total = total + swap(parts[at], distance, shards)
     else:
         gathered = lax.all_gather(own, "corpus", axis=0)
         decoded, rows = decode(pq_codes, codebook, full_rows)

time: 35.3 us -> 34.9 us (0.989)
  Pallas kernels: 11.2 us -> 10.4 us
  waiting for transfers between devices: 5.89 us -> 6.35 us
    pallas_call x1, Pallas kernels: 3.69 us -> 2.9 us  [decode(): pl.pallas_call(functools.partial(decode_kernel, step=step), out_shape=[pl...]
    ppermute x11, waiting for transfers between devices: 5.89 us -> 6.35 us  [swap(): return lax.ppermute(x, 'corpus', [(i, i ^ distance) for i in range(shards)])]
  transfers between devices with their start and end apart: 11 -> 11, of which waited for: 7 -> 6; matrix products, arithmetic and copies ran while one was open for 3% -> 3% of each run, Pallas kernels for 25% -> 23%
where the time goes in v4:
time: 34.9 us; the launch traced here: 34.7 us
  starting transfers between devices  15.6 us (45%)
  Pallas kernels  10.4 us (30%)
  waiting for transfers between devices  6.35 us (18%)
  local copies, waits for them, and re-layouts  1.06 us (3%)
  between operations  0.72 us (2%)
  other arithmetic  0.61 us (2%)
    ppermute x11, starting transfers between devices, swap(): return lax.ppermute(x, 'corpus', [(i, i ^ distance) for i in range(shards)])  15.6 us
    ppermute x11, waiting for transfers between devices, swap(): return lax.ppermute(x, 'corpus', [(i, i ^ distance) for i in range(shards)])  6.35 us
    pallas_call x2, Pallas kernels, exact(): pl.pallas_call(functools.partial(exact_kernel, per_query=per_query, group...  3.05 us
    pallas_call x1, Pallas kernels, decode(): pl.pallas_call(functools.partial(decode_kernel, step=step), out_shape=[pl...  2.9 us
    pallas_call x1, Pallas kernels, late_approx(): pl.pallas_call(functools.partial(late_approx_kernel, places=places, sub_w...  2.08 us
    pallas_call x1, Pallas kernels, score_blocks(): pl.pallas_call(functools.partial(scores_kernel, sub_width=sub_width), out...  1.41 us
    unnamed x5, local copies, waits for them, and re-layouts  0.98 us
    pallas_call x1, Pallas kernels, pack(): pl.pallas_call(functools.partial(pack_kernel, row_count=row_count), out_s...  0.95 us
  transfers between devices with their start and end apart: 11, of which 6 were waited for; matrix products, arithmetic and copies ran while one was open for 3% of the time, Pallas kernels for 23%

profile of v4, /device:TPU:0, one launch (start us, length us, event | category | flops | bytes accessed | tf_op | source)
XLA Modules:
  0.0 34.7 jit_solution(17304201698892861797)
XLA Ops:
  0.6 0.9 %pack.1.refs_0_ = bf16[528,128]{1,0:T(8,128)(2,1)S(1)} custom-call(bf16[64,1024]{1,0:T(8,128)(2,1)} %queries_ref.1, s32[16,64]{1,0:T(8,128)} %bitcast.19, s32[16,64]{1,0:T(8,128)} %bitcast.20), custom_call_target="tpu_custom_call" | custom-call | tf_op jit(solution)/shard_map/pack/pallas_call | solution.py:79
  1.6 4.1 %collective-permute-start = (bf16[528,128]{1,0:T(8,128)(2,1)S(1)}, bf16[528,128]{1,0:T(8,128)(2,1)S(1)}, u32[]{:S(2)}, u32[]{:S(2)}) collective-permute-start(bf16[528,128]{1,0:T(8,128)(2,1)S(1)} %pack.1.refs_0_), channel_id=1, source_target_pairs={{0,8},{2,10},{4,12},{6,14},{8,0},{10,2},{12,4},{14,6},{1,9},{3,11}... | collective-permute-start | bytes 405512 | tf_op jit(solution)/shard_map/ppermute | solution.py:344
  5.7 2.5 %collective-permute-start.6 = (bf16[528,128]{1,0:T(8,128)(2,1)S(1)}, bf16[528,128]{1,0:T(8,128)(2,1)S(1)}, u32[]{:S(2)}, u32[]{:S(2)}) collective-permute-start(bf16[528,128]{1,0:T(8,128)(2,1)S(1)} %pack.1.refs_0_), channel_id=1, source_target_pairs={{0,6},{2,4},{4,2},{6,0},{8,14},{10,12},{12,10},{14,8},{1,7},{3,5},... | collective-permute-start | bytes 405512 | tf_op jit(solution)/shard_map/ppermute | solution.py:344
  8.2 0.5 %collective-permute-start.5 = (bf16[528,128]{1,0:T(8,128)(2,1)S(1)}, bf16[528,128]{1,0:T(8,128)(2,1)S(1)}, u32[]{:S(2)}, u32[]{:S(2)}) collective-permute-start(bf16[528,128]{1,0:T(8,128)(2,1)S(1)} %pack.1.refs_0_), channel_id=1, source_target_pairs={{0,2},{2,0},{4,6},{6,4},{8,10},{10,8},{12,14},{14,12},{1,3},{3,1},... | collective-permute-start | bytes 405512 | tf_op jit(solution)/shard_map/ppermute | solution.py:344
  8.7 0.4 %collective-permute-start.4 = (bf16[528,128]{1,0:T(8,128)(2,1)S(1)}, bf16[528,128]{1,0:T(8,128)(2,1)S(1)}, u32[]{:S(2)}, u32[]{:S(2)}) collective-permute-start(bf16[528,128]{1,0:T(8,128)(2,1)S(1)} %pack.1.refs_0_), channel_id=1, source_target_pairs={{0,4},{2,6},{4,0},{6,2},{8,12},{10,14},{12,8},{14,10},{1,5},{3,7},... | collective-permute-start | bytes 405512 | tf_op jit(solution)/shard_map/ppermute | solution.py:344
  9.2 2.9 %decode.1 = (bf16[2048,1024]{1,0:T(8,128)(2,1)S(1)}, bf16[2048,1024]{1,0:T(8,128)(2,1)S(1)}) custom-call(s32[2048,256]{1,0:T(8,128)} %codes_ref.1, bf16[16,1024]{1,0:T(8,128)(2,1)} %book_ref.1, bf16[2048,1024]{1,0:T(8,128)(2,1)} %rows_ref.1), custom_call_target="tpu_custom_call" | custom-call | tf_op jit(solution)/shard_map/decode/pallas_call | solution.py:153
  12.1 2.4 %collective-permute-start.3 = (bf16[528,128]{1,0:T(8,128)(2,1)S(1)}, bf16[528,128]{1,0:T(8,128)(2,1)S(1)}, u32[]{:S(2)}, u32[]{:S(2)}) collective-permute-start(bf16[528,128]{1,0:T(8,128)(2,1)S(1)} %pack.1.refs_0_), channel_id=1, source_target_pairs={{0,14},{2,12},{4,10},{6,8},{8,6},{10,4},{12,2},{14,0},{1,15},{3,13... | collective-permute-start | bytes 405512 | tf_op jit(solution)/shard_map/ppermute | solution.py:344
  14.5 0.0 collective-permute-done.refs_0_
  14.5 0.0 collective-permute-start.2
  14.5 0.0 collective-permute-done.6.refs_3_
  14.5 1.5 %collective-permute-start.1 = (bf16[528,128]{1,0:T(8,128)(2,1)S(1)}, bf16[528,128]{1,0:T(8,128)(2,1)S(1)}, u32[]{:S(2)}, u32[]{:S(2)}) collective-permute-start(bf16[528,128]{1,0:T(8,128)(2,1)S(1)} %collective-permute-done.refs_0_), channel_id=1, source_target_pairs={{0,2},{2,0},{4,6},{6,4},{8,10},{10,8},{12,14},{14,12},{1,3},{3,1},... | collective-permute-start | bytes 405512 | tf_op jit(solution)/shard_map/ppermute | solution.py:344
  15.9 0.0 collective-permute-done.5.refs_2_
  15.9 2.6 %collective-permute-done.4.refs_1_ = bf16[528,128]{1,0:T(8,128)(2,1)S(1)} collective-permute-done((bf16[528,128]{1,0:T(8,128)(2,1)S(1)}, bf16[528,128]{1,0:T(8,128)(2,1)S(1)}, u32[]{:S(2)}, u32[]{:S(2)}) %collective-permute-start.4) | collective-permute-done | bytes 135200 | tf_op jit(solution)/shard_map/ppermute | solution.py:344
  18.5 1.5 %exact.2 = f32[16,256]{1,0:T(8,128)S(1)} custom-call(bf16[2048,1024]{1,0:T(8,128)(2,1)S(1)} %get-tuple-element.19.rows_ref, bf16[528,128]{1,0:T(8,128)(2,1)S(1)} %pack.1.refs_0_, bf16[528,128]{1,0:T(8,128)(2,1)S(1)} %collective-permute-done.4.refs_1_, bf16[528,128]{1,0:T(8,128)(2,1)S(1)} %collective-permute-done.5.refs_2_, ...), custom_call_target="tpu_custom_call" | custom-call | tf_op jit(solution)/shard_map/exact/pallas_call | solution.py:252
  20.0 0.0 copy-start
  20.0 0.0 copy-start.1
  20.1 1.4 %score_blocks.1.scores_ref = bf16[8,256,256]{2,1,0:T(8,128)(2,1)S(1)} custom-call(bf16[2048,1024]{1,0:T(8,128)(2,1)S(1)} %get-tuple-element.20.decoded_ref, bf16[528,128]{1,0:T(8,128)(2,1)S(1)} %pack.1.refs_0_, bf16[528,128]{1,0:T(8,128)(2,1)S(1)} %collective-permute-done.4.refs_1_, bf16[528,128]{1,0:T(8,128)(2,1)S(1)} %collective-permute-done.5.refs_2_, ...), custom_call_target="tpu_custom_call" | custom-call | tf_op jit(solution)/shard_map/score_blocks/pallas_call | solution.py:273
  21.5 0.0 collective-permute-done.3.refs_3_
  21.5 0.6 %collective-permute-done.2.refs_1_ = bf16[528,128]{1,0:T(8,128)(2,1)S(1)} collective-permute-done((bf16[528,128]{1,0:T(8,128)(2,1)S(1)}, bf16[528,128]{1,0:T(8,128)(2,1)S(1)}, u32[]{:S(2)}, u32[]{:S(2)}) %collective-permute-start.2) | collective-permute-done | bytes 135200 | tf_op jit(solution)/shard_map/ppermute | solution.py:344
  22.1 0.0 collective-permute-done.1.refs_2_
  22.1 1.5 %exact.3 = f32[16,256]{1,0:T(8,128)S(1)} custom-call(bf16[2048,1024]{1,0:T(8,128)(2,1)S(1)} %get-tuple-element.19.rows_ref, bf16[528,128]{1,0:T(8,128)(2,1)S(1)} %collective-permute-done.refs_0_, bf16[528,128]{1,0:T(8,128)(2,1)S(1)} %collective-permute-done.2.refs_1_, bf16[528,128]{1,0:T(8,128)(2,1)S(1)} %collective-permute-done.1.refs_2_, ...), custom_call_target="tpu_custom_call" | custom-call | tf_op jit(solution)/shard_map/exact/pallas_call | solution.py:252
  23.6 0.7 %collective-permute-start.7 = (f32[16,256]{1,0:T(8,128)S(1)}, f32[16,256]{1,0:T(8,128)S(1)}, u32[]{:S(2)}, u32[]{:S(2)}) collective-permute-start(f32[16,256]{1,0:T(8,128)S(1)} %exact.3), channel_id=1, source_target_pairs={{0,8},{2,10},{4,12},{6,14},{8,0},{10,2},{12,4},{14,6},{1,9},{3,11}... | collective-permute-start | bytes 49160 | tf_op jit(solution)/shard_map/ppermute | solution.py:344
  24.3 0.0 copy-done
  24.3 0.0 copy-done.1
  24.3 2.1 %late_approx.1 = bf16[8,4,64,256]{3,2,1,0:T(8,128)(2,1)S(1)} custom-call(s32[4,8]{1,0:T(4,128)S(1)} %bitcast.17, s32[8]{0:T(128)S(1)} %bitcast.18, bf16[2048,1024]{1,0:T(8,128)(2,1)S(1)} %get-tuple-element.20.decoded_ref, bf16[8,256,256]{2,1,0:T(8,128)(2,1)S(1)} %score_blocks.1.scores_ref, bf16[528,128]{1,0:T(8,128)(2,1)S(1)} %collective-permute-done.refs_0_, ...), custom_call_target="tpu_custom_call" | custom-call | flops 10000000000 | bytes 10485760 | tf_op jit(solution)/shard_map/late_approx/pallas_call | solution.py:311
  26.4 2.1 %collective-permute-done.7 = f32[16,256]{1,0:T(8,128)S(1)} collective-permute-done((f32[16,256]{1,0:T(8,128)S(1)}, f32[16,256]{1,0:T(8,128)S(1)}, u32[]{:S(2)}, u32[]{:S(2)}) %collective-permute-start.7) | collective-permute-done | bytes 16416 | tf_op jit(solution)/shard_map/ppermute | solution.py:344
  28.5 0.1 fusion
  28.6 1.3 %collective-permute-start.8 = (f32[16,64]{1,0:T(8,128)S(1)}, f32[16,64]{1,0:T(8,128)S(1)}, u32[]{:S(2)}, u32[]{:S(2)}) collective-permute-start(f32[16,64]{1,0:T(8,128)S(1)} %get-tuple-element.30), channel_id=1, source_target_pairs={{0,6},{2,4},{4,2},{6,0},{8,14},{10,12},{12,10},{14,8},{1,7},{3,5},... | collective-permute-start | bytes 12296 | tf_op jit(solution)/shard_map/ppermute | solution.py:344
  29.9 0.6 %collective-permute-start.10 = (f32[16,64]{1,0:T(8,128)S(1)}, f32[16,64]{1,0:T(8,128)S(1)}, u32[]{:S(2)}, u32[]{:S(2)}) collective-permute-start(f32[16,64]{1,0:T(8,128)S(1)} %get-tuple-element.31), channel_id=1, source_target_pairs={{0,4},{2,6},{4,0},{6,2},{8,12},{10,14},{12,8},{14,10},{1,5},{3,7},... | collective-permute-start | bytes 12296 | tf_op jit(solution)/shard_map/ppermute | solution.py:344
  30.5 1.6 %collective-permute-start.9 = (f32[16,64]{1,0:T(8,128)S(1)}, f32[16,64]{1,0:T(8,128)S(1)}, u32[]{:S(2)}, u32[]{:S(2)}) collective-permute-start(f32[16,64]{1,0:T(8,128)S(1)} %get-tuple-element.32), channel_id=1, source_target_pairs={{0,2},{2,0},{4,6},{6,4},{8,10},{10,8},{12,14},{14,12},{1,3},{3,1},... | collective-permute-start | bytes 12296 | tf_op jit(solution)/shard_map/ppermute | solution.py:344
  32.1 1.0 %copy.11 = bf16[8,1,1,4,64,256]{5,4,3,2,1,0:T(8,128)(2,1)} copy(bf16[8,1,1,4,64,256]{5,4,3,2,1,0:T(8,128)(2,1)S(1)} %bitcast.16) | data formatting | bytes 2097152
  33.1 0.1 collective-permute-done.8
  33.2 0.4 %collective-permute-done.10 = f32[16,64]{1,0:T(8,128)S(1)} collective-permute-done((f32[16,64]{1,0:T(8,128)S(1)}, f32[16,64]{1,0:T(8,128)S(1)}, u32[]{:S(2)}, u32[]{:S(2)}) %collective-permute-start.10) | collective-permute-done | bytes 4128 | tf_op jit(solution)/shard_map/ppermute | solution.py:344
  33.5 0.6 %collective-permute-done.9 = f32[16,64]{1,0:T(8,128)S(1)} collective-permute-done((f32[16,64]{1,0:T(8,128)S(1)}, f32[16,64]{1,0:T(8,128)S(1)}, u32[]{:S(2)}, u32[]{:S(2)}) %collective-permute-start.9) | collective-permute-done | bytes 4128 | tf_op jit(solution)/shard_map/ppermute | solution.py:344
  34.1 0.6 %add_add_fusion = f32[16,64]{1,0:T(8,128)} fusion(f32[16,64]{1,0:T(8,128)S(1)} %collective-permute-done.10, f32[16,64]{1,0:T(8,128)S(1)} %collective-permute-done.9, f32[16,64]{1,0:T(8,128)S(1)} %collective-permute-done.8, f32[16,256]{1,0:T(8,128)S(1)} %add.12), kind=kLoop, calls=%fused_computation | loop fusion | flops 3072 | bytes 20480 | tf_op jit(solution)/shard_map/add | solution.py:392
  (1 shorter events, 0.0 us)
Async XLA Ops:
  1.6 12.9 %collective-permute-start = (bf16[528,128]{1,0:T(8,128)(2,1)S(1)}, bf16[528,128]{1,0:T(8,128)(2,1)S(1)}, u32[]{:S(2)}, u32[]{:S(2)}) collective-permute-start(bf16[528,128]{1,0:T(8,128)(2,1)S(1)} %pack.1.refs_0_), channel_id=1, source_target_pairs={{0,8},{2,10},{4,12},{6,14},{8,0},{10,2},{12,4},{14,6},{1,9},{3,11}... | collective-permute-start | bytes 405512 | tf_op jit(solution)/shard_map/ppermute | solution.py:344
  5.7 8.8 %collective-permute-start.6 = (bf16[528,128]{1,0:T(8,128)(2,1)S(1)}, bf16[528,128]{1,0:T(8,128)(2,1)S(1)}, u32[]{:S(2)}, u32[]{:S(2)}) collective-permute-start(bf16[528,128]{1,0:T(8,128)(2,1)S(1)} %pack.1.refs_0_), channel_id=1, source_target_pairs={{0,6},{2,4},{4,2},{6,0},{8,14},{10,12},{12,10},{14,8},{1,7},{3,5},... | collective-permute-start | bytes 405512 | tf_op jit(solution)/shard_map/ppermute | solution.py:344
  8.2 7.7 %collective-permute-start.5 = (bf16[528,128]{1,0:T(8,128)(2,1)S(1)}, bf16[528,128]{1,0:T(8,128)(2,1)S(1)}, u32[]{:S(2)}, u32[]{:S(2)}) collective-permute-start(bf16[528,128]{1,0:T(8,128)(2,1)S(1)} %pack.1.refs_0_), channel_id=1, source_target_pairs={{0,2},{2,0},{4,6},{6,4},{8,10},{10,8},{12,14},{14,12},{1,3},{3,1},... | collective-permute-start | bytes 405512 | tf_op jit(solution)/shard_map/ppermute | solution.py:344
  8.7 9.8 %collective-permute-start.4 = (bf16[528,128]{1,0:T(8,128)(2,1)S(1)}, bf16[528,128]{1,0:T(8,128)(2,1)S(1)}, u32[]{:S(2)}, u32[]{:S(2)}) collective-permute-start(bf16[528,128]{1,0:T(8,128)(2,1)S(1)} %pack.1.refs_0_), channel_id=1, source_target_pairs={{0,4},{2,6},{4,0},{6,2},{8,12},{10,14},{12,8},{14,10},{1,5},{3,7},... | collective-permute-start | bytes 405512 | tf_op jit(solution)/shard_map/ppermute | solution.py:344
  12.1 9.4 %collective-permute-start.3 = (bf16[528,128]{1,0:T(8,128)(2,1)S(1)}, bf16[528,128]{1,0:T(8,128)(2,1)S(1)}, u32[]{:S(2)}, u32[]{:S(2)}) collective-permute-start(bf16[528,128]{1,0:T(8,128)(2,1)S(1)} %pack.1.refs_0_), channel_id=1, source_target_pairs={{0,14},{2,12},{4,10},{6,8},{8,6},{10,4},{12,2},{14,0},{1,15},{3,13... | collective-permute-start | bytes 405512 | tf_op jit(solution)/shard_map/ppermute | solution.py:344
  14.5 7.7 %collective-permute-start.2 = (bf16[528,128]{1,0:T(8,128)(2,1)S(1)}, bf16[528,128]{1,0:T(8,128)(2,1)S(1)}, u32[]{:S(2)}, u32[]{:S(2)}) collective-permute-start(bf16[528,128]{1,0:T(8,128)(2,1)S(1)} %collective-permute-done.refs_0_), channel_id=1, source_target_pairs={{0,4},{2,6},{4,0},{6,2},{8,12},{10,14},{12,8},{14,10},{1,5},{3,7},... | collective-permute-start | bytes 405512 | tf_op jit(solution)/shard_map/ppermute | solution.py:344
  14.5 7.6 %collective-permute-start.1 = (bf16[528,128]{1,0:T(8,128)(2,1)S(1)}, bf16[528,128]{1,0:T(8,128)(2,1)S(1)}, u32[]{:S(2)}, u32[]{:S(2)}) collective-permute-start(bf16[528,128]{1,0:T(8,128)(2,1)S(1)} %collective-permute-done.refs_0_), channel_id=1, source_target_pairs={{0,2},{2,0},{4,6},{6,4},{8,10},{10,8},{12,14},{14,12},{1,3},{3,1},... | collective-permute-start | bytes 405512 | tf_op jit(solution)/shard_map/ppermute | solution.py:344
  20.0 4.3 %copy-start = (s32[8,1,1,4]{0,3,2,1:T(4,128)S(1)}, s32[8,1,1,4]{0,3,2,1:T(4,128)}, u32[]{:S(2)}) copy-start(s32[8,1,1,4]{0,3,2,1:T(4,128)} %param.12) | copy-start | bytes 388
  20.0 4.3 %copy-start.1 = (s32[8,1,1]{0,2,1:T(1,128)S(1)}, s32[8,1,1]{0,2,1:T(1,128)}, u32[]{:S(2)}) copy-start(s32[8,1,1]{0,2,1:T(1,128)} %param.13) | copy-start | bytes 100
  23.6 4.9 %collective-permute-start.7 = (f32[16,256]{1,0:T(8,128)S(1)}, f32[16,256]{1,0:T(8,128)S(1)}, u32[]{:S(2)}, u32[]{:S(2)}) collective-permute-start(f32[16,256]{1,0:T(8,128)S(1)} %exact.3), channel_id=1, source_target_pairs={{0,8},{2,10},{4,12},{6,14},{8,0},{10,2},{12,4},{14,6},{1,9},{3,11}... | collective-permute-start | bytes 49160 | tf_op jit(solution)/shard_map/ppermute | solution.py:344
  28.6 4.6 %collective-permute-start.8 = (f32[16,64]{1,0:T(8,128)S(1)}, f32[16,64]{1,0:T(8,128)S(1)}, u32[]{:S(2)}, u32[]{:S(2)}) collective-permute-start(f32[16,64]{1,0:T(8,128)S(1)} %get-tuple-element.30), channel_id=1, source_target_pairs={{0,6},{2,4},{4,2},{6,0},{8,14},{10,12},{12,10},{14,8},{1,7},{3,5},... | collective-permute-start | bytes 12296 | tf_op jit(solution)/shard_map/ppermute | solution.py:344
  29.9 3.7 %collective-permute-start.10 = (f32[16,64]{1,0:T(8,128)S(1)}, f32[16,64]{1,0:T(8,128)S(1)}, u32[]{:S(2)}, u32[]{:S(2)}) collective-permute-start(f32[16,64]{1,0:T(8,128)S(1)} %get-tuple-element.31), channel_id=1, source_target_pairs={{0,4},{2,6},{4,0},{6,2},{8,12},{10,14},{12,8},{14,10},{1,5},{3,7},... | collective-permute-start | bytes 12296 | tf_op jit(solution)/shard_map/ppermute | solution.py:344
  30.5 3.7 %collective-permute-start.9 = (f32[16,64]{1,0:T(8,128)S(1)}, f32[16,64]{1,0:T(8,128)S(1)}, u32[]{:S(2)}, u32[]{:S(2)}) collective-permute-start(f32[16,64]{1,0:T(8,128)S(1)} %get-tuple-element.32), channel_id=1, source_target_pairs={{0,2},{2,0},{4,6},{6,4},{8,10},{10,8},{12,14},{14,12},{1,3},{3,1},... | collective-permute-start | bytes 12296 | tf_op jit(solution)/shard_map/ppermute | solution.py:344
